TPU v7x, 32 devices: a whole 2x2x4 slice. The times are simulated.
32 devices in a mesh: parts: 2 (over y), row: 4 (over z), col: 2 (over x), depth: 2 (over core).
Axes of the slice: x: 2, y: 2, z: 4, core: 2. Of those that a mesh axis runs over, the one named last changes fastest.
Arguments:
- homolog_ensemble: bfloat16 [128, 64, 64], P(('parts', 'depth'), 'row'), parts along dimension 0, may hold values from -6 to 6
- duplex_embedding: bfloat16 [128, 64, 128], P(('parts', 'row'), 'col'), parts along dimension 0, may hold values from -6 to 6
- homolog_present_flags: int32 [128], P('parts'), parts along dimension 0, may hold values 0 or 1
- resolved_position_flags: int32 [128], P(('parts', 'col')), parts along dimension 0, may hold values 0 or 1
- payload_weights: bfloat16 [64, 256], replicated, may hold values from -0.75 to 0.75
- sigmoid_weights: bfloat16 [64, 256], replicated, may hold values from -0.75 to 0.75
- averager_final_weights: bfloat16 [256, 64], replicated, may hold values from -0.375 to 0.375
- first_operand_weights: bfloat16 [64, 32], replicated, may hold values from -0.75 to 0.75
- second_operand_weights: bfloat16 [64, 32], replicated, may hold values from -0.75 to 0.75
- duplex_logit_weights: bfloat16 [128, 8], replicated, may hold values from -20 to 20
- tensor_product_weights: bfloat16 [1024, 128], replicated, may hold values from -0.1875 to 0.1875
- averager_upstream_adjoint: bfloat16 [128, 64, 64], P(('parts', 'depth'), 'row'), parts along dimension 0, may hold values from -6 to 6
- duplex_upstream_adjoint: bfloat16 [128, 64, 128], P(('parts', 'row'), 'col'), parts along dimension 0, may hold values from -2.5 to 2.5
Outputs:
- ensemble_derivative: bfloat16 [128, 64, 64], P(('parts', 'depth'), 'row'), parts along dimension 0
- pairwise_gradient: bfloat16 [128, 64, 128], P(('parts', 'row'), 'col'), parts along dimension 0
- outer_matrix_gradient: float32 [2048, 128], P('parts'), parts along dimension 0
There are 2 independent parts, one for each index of `parts`. A program takes and returns all parts, laid end to end along the dimension named above; an argument that names none is the same for every part. Nothing has to cross between parts.
All inputs are finite; a program needn't handle non-finite values. No bound on the sum of `resolved_position_flags` on one device may be relied on, other than what follows from the above.
Results may differ from a plain program's by a relative error of at most 0.013.
The roundings to bfloat16 on the way count: a program that leaves them out, or rounds other values in their place, can miss the bound.
Values may be sent and summed in bfloat16 or wider, within the bound.
No kernel may reach another device: no remote copies, remote signals or barrier semaphores. Data moves between devices by JAX's collectives and lax.ppermute only.
A program may use at most 64 MiB of HBM per device.

v0:
```python
import functools
import math

import jax
import jax.numpy as jnp
from jax import lax
from jax.experimental import pallas as pl
from jax.experimental.pallas import tpu as pltpu
from jax.sharding import PartitionSpec as P

EPS = 1e-05
PENALTY = 10000.0
F32 = jnp.float32
BF16 = jnp.bfloat16
LANES = 128
NN = (((1,), (0,)), ((), ()))
NT = (((1,), (1,)), ((), ()))
VMEM = pl.BlockSpec(memory_space=pltpu.VMEM)
FAR = pl.BlockSpec(memory_space=pl.ANY)


def mm(a, b, dims=NN):
    return lax.dot_general(a, b, dims, preferred_element_type=F32)


def split_high_low(value):
    high = value.astype(BF16)
    return high, (value - high.astype(F32)).astype(BF16)


def iota(shape, dim):
    return lax.broadcasted_iota(jnp.int32, shape, dim)


def lanes_of(pieces):
    return pieces[0] if len(pieces) == 1 else jnp.concatenate(pieces, axis=-1)


def rows_of(pieces):
    return pieces[0] if len(pieces) == 1 else jnp.concatenate(pieces, axis=0)


def standardize(values):
    centred = values - jnp.mean(values, -1, keepdims=True)
    inverse = lax.rsqrt(jnp.mean(centred * centred, -1, keepdims=True) + EPS)
    return centred * inverse, inverse


def standardize_backward(values, upstream):
    scaled, inverse = standardize(values)
    mean_grad = jnp.mean(upstream, -1, keepdims=True)
    mean_cross = jnp.mean(upstream * scaled, -1, keepdims=True)
    return (upstream - mean_grad - scaled * mean_cross) * inverse


def on_diagonal(block, width):
    rows, lanes = block.shape
    same = iota(block.shape, 0) // (rows // 2) == iota(block.shape, 1) // width
    return jnp.where(same, block, jnp.zeros_like(block))


def split_three(value):
    high = value.astype(BF16)
    rest = value - high.astype(F32)
    middle = rest.astype(BF16)
    return [high, middle, (rest - middle.astype(F32)).astype(BF16)]


def three_lanes(value):
    rows, width = value.shape
    fill = -(3 * width) % LANES
    return lanes_of(split_three(value) + [jnp.zeros((rows, fill), BF16)] * (fill > 0))


def join_three(parts, width):
    wide = parts.astype(F32)
    return (wide[:, :width] + wide[:, width : 2 * width]) + wide[:, 2 * width : 3 * width]


def twice(weights):
    zero = jnp.zeros_like(weights)
    return rows_of([lanes_of([weights, zero]), lanes_of([zero, weights])])


def column_weights(g, w2):
    rows = iota((2 * g.QL, g.Q), 0) % g.QL + lax.axis_index("col") * g.QL
    pick = (iota((2 * g.QL, g.Q), 1) == rows).astype(BF16)
    return on_diagonal(mm(pick, lanes_of([w2, w2])), g.M).astype(BF16)


def normalise_kernel(
    g, x_hbm, e_hbm, dd_hbm, flag_hbm, wl_hbm, live_hbm, w1_hbm, t_hbm, w2_hbm, *refs
):
    xn_ref, send_ref, logit_ref, near_ref, x_ref, e_ref, wl_ref, mask_ref, w1_ref, t_ref, w2_ref = refs[:11]
    flag_in, live_in, x_in, norm_ref, rows_ref, sem = refs[11:]
    col = lax.axis_index("col")
    pairs = g.I * g.JC
    copies = [
        pltpu.make_async_copy(a, b, sem.at[k])
        for k, (a, b) in enumerate(
            [
                (x_hbm, x_in),
                (e_hbm, e_ref),
                (wl_hbm, wl_ref),
                (flag_hbm, flag_in),
                (dd_hbm, near_ref.at[pl.ds(0, pairs)]),
                (live_hbm, live_in),
                (w1_hbm, w1_ref),
                (t_hbm, t_ref),
                (w2_hbm, w2_ref),
            ]
        )
    ]
    for copy in copies:
        copy.start()
    copies[5].wait()
    lane = iota((1, 2 * g.M), 1)
    groups = [lax.rem(col + m, g.C) for m in range(g.C)]
    for m, group in enumerate(groups):
        first = (lax.axis_index("depth") * g.C + group) * g.SQ
        for k in range(g.SP):
            if 2 * k + 1 < g.SQ:
                flags = jnp.where(lane < g.M, live_in[first + 2 * k], live_in[first + 2 * k + 1])
                flags = flags.astype(F32)
            else:
                flags = jnp.zeros((1, 2 * g.M), F32)
            mask_ref[m * g.SP + k : m * g.SP + k + 1, :] = flags
    total = live_in[0]
    for k in range(1, live_in.shape[0]):
        total = total + live_in[k]
    count = jnp.full((1, 2 * g.M), total, jnp.int32).astype(F32)
    mask_ref[g.C * g.SP : g.C * g.SP + 1, :] = 1.0 / (0.001 + count)
    copies[0].wait()
    copies[8].wait()
    norm_ref[...] = standardize(x_in[...].astype(F32))[0]
    x_ref[...] = x_in[pl.ds(col * g.SQ, g.SQ)]
    second = column_weights(g, w2_ref[...])
    rows, blocks = g.SP * g.I, []
    for m, group in enumerate(groups):
        normed = g.fill(norm_ref[pl.ds(group * g.SQ, g.SQ)]).reshape(g.SP, 2, g.I, g.M)
        packed = jnp.concatenate([normed[:, 0], normed[:, 1]], axis=-1).astype(BF16)
        xn_ref[m] = packed
        if m == 0:
            send_ref[:rows, :] = packed.reshape(rows, 2 * g.M)
        else:
            masks = [mask_ref[m * g.SP + k : m * g.SP + k + 1, :] for k in range(g.SP)]
            live = rows_of([(packed[k].astype(F32) * masks[k]).astype(BF16) for k in range(g.SP)])
            factors = mm(live, second, NT)
            blocks += [factors[k * g.I : (k + 1) * g.I] for k in range(g.SP)]
    if blocks:
        wide = lanes_of(blocks)
        fill = -wide.shape[1] % LANES
        if fill:
            wide = lanes_of([wide, jnp.zeros((g.I, fill), F32)])
        for k in range(g.EXTRA):
            block = wide[:, k * LANES : (k + 1) * LANES]
            send_ref[rows + k * g.I : rows + (k + 1) * g.I, :] = block.astype(BF16)
    for copy in copies[1:4]:
        copy.wait()
    pair = standardize(e_ref[...].astype(F32).reshape(pairs, g.Z))[0].astype(BF16)
    penalty = (flag_in[...].astype(F32) - 1.0) * PENALTY
    weights = wl_ref[...]
    for i in range(g.I):
        rows_ref[i * g.H : (i + 1) * g.H, : g.JC] = (
            mm(weights, pair[i * g.JC : (i + 1) * g.JC], NT) + penalty
        )
    logits = rows_of([rows_ref[pl.ds(h, g.I, stride=g.H), :][:, : g.JC] for h in range(g.H)])
    tall = g.H * g.I // g.G
    packed = lanes_of([logits[k * tall : (k + 1) * tall] for k in range(g.G)])
    logit_ref[...] = packed
    near_ref[pairs:, :] = rows_of(split_three(packed))
    for copy in (copies[4], *copies[6:8]):
        copy.wait()


def prepare_kernel(g, xn_ref, w1_ref, t_ref, mask_ref, u_hbm, *refs):
    refs = list(refs)
    count = g.carried
    sources, refs = refs[:count], refs[count:]
    left_ref, ts_ref, lt_ref, u_ref, refs = refs[0], refs[1], refs[2], refs[3], refs[4:]
    targets, (wide_ref, half_ref, first_sem, later_sem) = refs[:count], refs[count:]
    first = lax.axis_index("col") * g.SQ
    copies = [pltpu.make_async_copy(u_hbm.at[pl.ds(first, g.SQ)], u_ref, first_sem)]
    copies += [
        pltpu.make_async_copy(a, b, later_sem.at[k])
        for k, (a, b) in enumerate(zip(sources, targets, strict=True))
    ]
    for copy in copies:
        copy.start()
    w1 = rows_of([w1_ref[...], jnp.zeros((LANES - g.Q, g.M), BF16)])
    zero = jnp.zeros_like(w1)
    for m in range(g.C):
        masks = [mask_ref[m * g.SP + k : m * g.SP + k + 1, :] for k in range(g.SP)]
        live_xn = rows_of(
            [(xn_ref[m, k].astype(F32) * masks[k]).astype(BF16) for k in range(g.SP)]
        )
        half_ref[0] = mm(live_xn, lanes_of([w1, zero]), NT)
        half_ref[1] = mm(live_xn, lanes_of([zero, w1]), NT)
        for i in range(g.I):
            halves = [half_ref[half, pl.ds(i, g.SP, stride=g.I), :] for half in range(2)]
            first = (m * g.I + i) * g.S
            left_ref[first : first + g.S, :] = rows_of(halves)[:, : g.Q].astype(BF16)
    wide_ref[...] = t_ref[...].astype(F32)
    for q in range(g.Q):
        ts_ref[q] = wide_ref[pl.ds(q, g.Q, stride=g.Q), :].astype(BF16)
    left = left_ref[: g.I * g.S, :]
    for q in range(0, g.Q, 2):
        product = mm(left, lanes_of([ts_ref[q], ts_ref[q + 1]]))
        for k in range(2):
            block = product[:, k * g.Z : (k + 1) * g.Z].reshape(g.I, g.S, g.Z)
            lt_ref[:, (q + k) * g.S : (q + k + 1) * g.S, :] = block.astype(BF16)
    for copy in copies:
        copy.wait()


def gate_kernel(g, xn_ref, u_ref, sg_ref, wf_ref, gate_weight_ref, gm_ref, gate_ref):
    rows = g.SP * g.I
    xn = xn_ref[0]
    gate_weights = twice(sg_ref[...])
    gate_weight_ref[...] = gate_weights
    gates = jax.nn.sigmoid(mm(xn.reshape(rows, 2 * g.M), gate_weights))
    u = g.fill(u_ref[...]).reshape(g.SP, 2, g.I, g.M)
    packed_u = jnp.concatenate([u[:, 0], u[:, 1]], axis=-1).reshape(rows, 2 * g.M)
    gated = mm(packed_u, twice(wf_ref[...]))
    blended = gated * gates
    gm_ref[...] = blended.astype(BF16)
    gate_ref[...] = blended * (1.0 - gates)


def right_kernel(g, *refs):
    near_refs, (lt_ref, w2_ref, mask_ref, d_ref, go_ref, rg_ref) = refs[: g.C], refs[g.C :]
    for k in range(g.C):
        spot = (g.C - k) % g.C
        block = near_refs[k][: g.I * g.JC, :].reshape(g.I, g.JC, g.Z)
        d_ref[:, spot * g.JC : (spot + 1) * g.JC, :] = block
    masks = [mask_ref[k : k + 1, :] for k in range(g.SP)]
    scale = mask_ref[g.C * g.SP : g.C * g.SP + 1, :]
    right_grad = jnp.zeros((g.Q * g.S, g.N), F32)
    for i in range(0, g.I, 2):
        right_grad = right_grad + mm(
            lanes_of([lt_ref[i], lt_ref[i + 1]]), lanes_of([d_ref[i], d_ref[i + 1]]), NT
        )
    for t in range(g.NT):
        lanes = min(LANES, g.N - t * LANES)
        piece = right_grad[:, t * LANES : t * LANES + lanes]
        if lanes < LANES:
            piece = lanes_of([piece, jnp.zeros((g.Q * g.S, LANES - lanes), F32)])
        rg_ref[t] = piece
    deep = 2 * g.Q
    group = min(g.SP, LANES // deep)
    which = iota((group * deep, g.Q), 0)
    pick = (iota((group * deep, g.Q), 1) == which % deep // 2).astype(BF16)
    w2 = w2_ref[...]
    base = mm(pick, lanes_of([w2, w2]))
    which = iota(base.shape, 0)
    base = jnp.where(which % 2 == iota(base.shape, 1) // g.M, base, 0.0)
    weights = lanes_of([jnp.where(which // deep == k, base, 0.0) for k in range(group)]).astype(BF16)
    for k in range(0, g.SP, group):
        for t in range(g.NT):
            lanes = min(LANES, g.N - t * LANES)
            tall = rows_of(
                [rg_ref[t, pl.ds(k + m, deep, stride=g.SP), :] for m in range(group)]
            )
            tall = (tall * scale).T[:lanes]
            high, low = split_high_low(tall)
            part = mm(high, weights) + mm(low, weights)
            for m in range(group):
                go_ref[k + m, t * LANES : t * LANES + lanes, :] = (
                    part[:, m * 2 * g.M : (m + 1) * 2 * g.M] * masks[k + m]
                )


def outer_kernel(g, *refs):
    refs = list(refs)
    x_refs, refs = refs[: g.R], refs[g.R :]
    d_ref, left_ref, w2_ref, mask_ref, xall_ref, *refs = refs
    w_refs, (others_ref, spread_ref, rt_ref, ds_ref, all_ref) = refs[: g.D], refs[g.D :]
    row, col, depth = (lax.axis_index(a) for a in ("row", "col", "depth"))
    rows, deep = g.SP * g.I, 2 * g.QL
    for k, ref in zip((0, *g.order), x_refs, strict=True):
        place = g.place(jnp.bitwise_xor(row, k), col)
        xall_ref[:, pl.ds(place, g.I), :] = ref[:rows, :].reshape(g.SP, g.I, 2 * g.M)
        for m in range(g.EXTRA):
            block = ref[rows + m * g.I : rows + (m + 1) * g.I, :]
            others_ref[pl.ds(place, g.I), m * LANES : (m + 1) * LANES] = block
    second = column_weights(g, w2_ref[...])
    parts = [
        mm(second, (xall_ref[k].astype(F32) * mask_ref[k : k + 1, :]).astype(BF16), NT)
        for k in range(g.SP)
    ]
    if g.EXTRA:
        lanes = g.EXTRA * LANES
        eye = (iota((lanes, lanes), 0) == iota((lanes, lanes), 1)).astype(BF16)
        parts.append(mm(eye, others_ref[...], NT)[: (g.C - 1) * g.SP * deep])
    first = 0
    for part in parts:
        for t in range(g.NT):
            lanes = min(LANES, g.N - t * LANES)
            piece = part[:, t * LANES : t * LANES + lanes]
            spread_ref[t, first : first + part.shape[0], :lanes] = piece
        first += part.shape[0]
    for q in range(g.QL):
        for m in range(g.C):
            spot = (q * g.C + m) * g.S
            for t in range(g.NT):
                lanes = min(LANES, g.N - t * LANES)
                halves = [
                    spread_ref[t, pl.ds(m * g.SP * deep + half * g.QL + q, g.SP, stride=deep), :]
                    for half in range(2)
                ]
                rt_ref[spot : spot + g.S, t * LANES : t * LANES + lanes] = rows_of(halves)[
                    :, :lanes
                ].astype(BF16)
    rt = rt_ref[...]
    for i in range(0, g.I, 2):
        product = mm(rt, lanes_of([d_ref[i], d_ref[i + 1]]))
        for k in range(2):
            block = product[:, k * g.Z : (k + 1) * g.Z]
            ds_ref[:, :, i + k] = block.reshape(g.QL, g.C, g.S, g.Z).astype(BF16)
    eye = (iota((g.Q, g.Q), 0) == iota((g.Q, g.Q), 1)).astype(BF16)
    left_t = mm(eye, left_ref[...], NT).astype(BF16)
    scale = mask_ref[g.C * g.SP : g.C * g.SP + 1, :]
    entries = g.C * g.S * g.I
    for q in range(0, g.QL, 2):
        both = lanes_of([ds_ref[q].reshape(entries, g.Z), ds_ref[q + 1].reshape(entries, g.Z)])
        part = mm(left_t, both)
        all_ref[pl.ds(q, g.Q, stride=g.QL), :] = part[:, : g.Z] * scale
        all_ref[pl.ds(q + 1, g.Q, stride=g.QL), :] = part[:, g.Z :] * scale
    share = g.Q * g.QL // g.D
    for k in range(g.D):
        first = pl.multiple_of(lax.rem(depth + k, g.D) * share, share)
        w_refs[k][...] = all_ref[pl.ds(first, share), :]


def own_kernel(
    g, xall_ref, d_ref, ts_ref, w1_ref, w2_ref, mask_ref, part_ref, gg_ref, gate_weight_ref, own_ref,
    spread_ref, rt_ref, ds_ref, turn_ref,
):
    scale = mask_ref[g.C * g.SP : g.C * g.SP + 1, :]
    masks = [mask_ref[k : k + 1, :] for k in range(g.SP)]
    w2 = w2_ref[...]
    doubled = lanes_of([w2, w2])
    second = on_diagonal(rows_of([doubled, doubled]), g.M)
    for k in range(g.SP):
        live_x = (xall_ref[k].astype(F32) * masks[k]).astype(BF16)
        part = mm(second, live_x, NT)
        for t in range(g.NT):
            lanes = min(LANES, g.N - t * LANES)
            spread_ref[t, k * 2 * g.Q : (k + 1) * 2 * g.Q, :lanes] = part[
                :, t * LANES : t * LANES + lanes
            ]
    for q in range(g.Q):
        for t in range(g.NT):
            lanes = min(LANES, g.N - t * LANES)
            halves = [
                spread_ref[t, pl.ds(half * g.Q + q, g.SP, stride=2 * g.Q), :] for half in range(2)
            ]
            rt_ref[q * g.S : (q + 1) * g.S, t * LANES : t * LANES + lanes] = rows_of(halves)[
                :, :lanes
            ].astype(BF16)
    rt = rt_ref[...]
    for i in range(0, g.I, 2):
        product = mm(rt, lanes_of([d_ref[i], d_ref[i + 1]]))
        for k in range(2):
            block = product[:, k * g.Z : (k + 1) * g.Z]
            ds_ref[:, i + k] = block.reshape(g.Q, g.S, g.Z).astype(BF16)
    entries = g.S * g.I
    left_grad = jnp.zeros((entries, g.Q), F32)
    for q in range(0, g.Q, 2):
        both = lanes_of([ds_ref[q].reshape(entries, g.Z), ds_ref[q + 1].reshape(entries, g.Z)])
        left_grad = left_grad + mm(both, lanes_of([ts_ref[q], ts_ref[q + 1]]), NT)
    w1 = w1_ref[...]
    first_term = jnp.zeros((entries, 2 * g.M), F32)
    for piece in split_high_low(left_grad * scale[:, : g.Q]):
        first_term = first_term + mm(piece, lanes_of([w1, w1]))
    turn_ref[...] = first_term
    gate_term = mm(gg_ref[...], gate_weight_ref[...], NT)
    lane = iota((1, 2 * g.M), 1)
    for k in range(g.SP):
        rows = slice(k * g.I, (k + 1) * g.I)
        halves = [turn_ref[pl.ds(half * g.SP + k, g.I, stride=g.S), :] for half in range(2)]
        term = jnp.where(lane < g.M, halves[0], halves[1]) * mask_ref[k : k + 1, :]
        own_ref[rows, :] = part_ref[rows, :] + gate_term[rows] + term


def attend_kernel(g, *refs):
    refs = list(refs)
    xall_ref, refs = refs[0], refs[1:]
    logit_ref, near_refs, refs = refs[0], refs[1 : g.C], refs[g.C :]
    gm_ref, gate_ref, p_ref, go_ref, soft_ref, gs_ref, own_ref, gg_ref, *refs = refs
    send_refs, (total_ref,) = refs[: g.R - 1], refs[g.R - 1 :]
    row, col = lax.axis_index("row"), lax.axis_index("col")
    tall, blocks = logit_ref.shape[0], [logit_ref[...]]
    for k in range(1, g.C):
        parts = near_refs[g.C - k - 1][g.I * g.JC :, :].astype(F32)
        blocks.append((parts[:tall] + parts[tall : 2 * tall]) + parts[2 * tall :])
    logits = lanes_of(
        [rows_of([b[:, k * g.JC : (k + 1) * g.JC] for k in range(g.G)]) for b in blocks]
    )
    shifted = jnp.exp(logits - jnp.max(logits, -1, keepdims=True))
    soft = shifted / jnp.sum(shifted, -1, keepdims=True)
    soft_ref[...] = soft
    low = soft.astype(BF16)
    eye = (iota((g.N, g.N), 0) == iota((g.N, g.N), 1)).astype(BF16)
    low_t = mm(eye, low, NT).astype(BF16)
    value_weights = twice(p_ref[...])
    values = mm(xall_ref[...].reshape(g.SP * g.N, 2 * g.M), value_weights).astype(BF16)
    wide = value_weights.shape[1]
    head = iota((1, wide), 1) % (wide // 2) // (wide // 2 // g.H)
    grad_soft = jnp.zeros((g.H * g.I, g.N), F32)
    for k in range(g.SP):
        v = values[k * g.N : (k + 1) * g.N]
        crossed = mm(low, v)
        mixed = jnp.where(head == 0, crossed[: g.I], 0.0)
        for h in range(1, g.H):
            mixed = jnp.where(head == h, crossed[h * g.I : (h + 1) * g.I], mixed)
        rows = slice(k * g.I, (k + 1) * g.I)
        gg_ref[rows, :] = (gate_ref[rows, :] * mixed).astype(BF16)
        blended = gm_ref[rows, :]
        by_head = rows_of(
            [jnp.where(head == h, blended, jnp.zeros_like(blended)) for h in range(g.H)]
        )
        grad_soft = grad_soft + mm(by_head, v, NT)
        part = go_ref[k]
        for piece in split_high_low(mm(low_t, by_head)):
            part = part + mm(piece, value_weights, NT)
        total_ref[k] = part
    gs_ref[...] = grad_soft
    own = total_ref[:, pl.ds(g.place(row, col), g.I), :]
    own_ref[...] = own.reshape(g.SP * g.I, 2 * g.M)
    for x in range(1, g.R):
        block = total_ref[:, pl.ds(g.place(jnp.bitwise_xor(row, x), col), g.I), :]
        send_refs[x - 1][...] = block.reshape(g.SP * g.I, 2 * g.M).astype(BF16)


def pack_kernel(g, *refs):
    refs = list(refs)
    sums, refs = refs[: g.R - 1], refs[g.R - 1 :]
    parts, refs = refs[: g.D], refs[g.D :]
    outs, own_ref = refs[: g.R - 1], refs[g.R - 1]
    total = parts[0][...]
    for ref in parts[1:]:
        total = total + ref[...]
    total, rows = total.astype(BF16), g.SP * g.I
    own_ref[...] = total
    for x in range(1, g.R):
        outs[x - 1][:rows, :] = sums[x - 1][...]
        outs[x - 1][rows:, :] = total


def piece_kernel(g, own_ref, *refs):
    out_ref, order_ref = refs[-2:]
    row, rows = lax.axis_index("row"), g.SP * g.I
    order_ref[row] = own_ref[...]
    for k in range(1, g.R):
        order_ref[jnp.bitwise_xor(row, g.R - k)] = refs[k - 1][rows:, :]
    total = order_ref[0].astype(F32)
    for r in range(1, g.R):
        total = total + order_ref[r].astype(F32)
    out_ref[...] = total.astype(BF16)


def score_kernel(g, soft_ref, *refs):
    parts, refs = refs[: g.D], refs[g.D :]
    own_ref, out_refs, order_ref = refs[0], refs[1 : g.C], refs[g.C]
    depth = lax.axis_index("depth")
    for k in range(g.D):
        order_ref[lax.rem(depth - k + g.D, g.D)] = parts[k][...]
    grad_soft = order_ref[0]
    for k in range(1, g.D):
        grad_soft = grad_soft + order_ref[k]
    inner = jnp.sum(soft_ref[...] * grad_soft, -1, keepdims=True)
    for k in range(g.C):
        block = lanes_of([grad_soft[:, k * g.JC : (k + 1) * g.JC], inner])
        if k == 0:
            own_ref[...] = block
        else:
            out_refs[k - 1][...] = three_lanes(block)


def pair_kernel(g, e_ref, wl_ref, soft_ref, own_ref, *refs):
    got, pair_ref = refs[: g.C - 1], refs[g.C - 1]
    heads = g.H * g.I
    total = own_ref[...]
    for ref in got:
        total = total + join_three(ref[...], g.JC + 1)
    grad = soft_ref[:, : g.JC] * (total[:, : g.JC] - total[:, g.JC :])
    if g.JC < LANES:
        grad = lanes_of([grad, jnp.zeros((heads, LANES - g.JC), F32)])
    high, low = split_high_low(grad.T[: g.JC])
    grads = lanes_of([high, low])
    pick = (iota((heads, g.H), 0) // g.I == iota((heads, g.H), 1)).astype(BF16)
    base = mm(pick, wl_ref[...]).astype(BF16)
    token = iota((heads, 1), 0) % g.I
    for i in range(0, g.I, 2):
        weights = lanes_of(
            [jnp.where(token == i + k, base, jnp.zeros_like(base)) for k in range(2)]
        )
        upstream = mm(grads, rows_of([weights, weights]))
        for k in range(2):
            pair_ref[i + k] = standardize_backward(
                e_ref[i + k].astype(F32), upstream[:, k * g.Z : (k + 1) * g.Z]
            ).astype(BF16)


def reduce_kernel(g, x_ref, own_ref, *refs):
    got, out_ref = refs[:-1], refs[-1]
    rows = g.SP * g.I
    total = own_ref[...]
    for ref in got:
        total = total + ref[:rows, :].astype(F32)
    total = total.reshape(g.SP, 1, g.I, 2 * g.M)
    upstream = jnp.concatenate([total[..., : g.M], total[..., g.M :]], axis=1)
    upstream = upstream.reshape(g.S, g.I, g.M)[: g.SQ]
    msa = g.fill(standardize_backward(x_ref[...].astype(F32), upstream))
    msa = msa.reshape(g.SP, 2, g.I, g.M)
    msa = jnp.concatenate([msa[:, 0], msa[:, 1]], axis=-1).astype(BF16)
    out_ref[...] = msa.reshape(rows, 2 * g.M)


def across_kernel(g, *refs):
    out_ref = refs[-1]
    col = lax.axis_index("col")
    for k, ref in enumerate(refs[:-1]):
        out_ref[lax.rem(col - k + g.C, g.C)] = ref[...]


def unpack_kernel(g, *refs):
    parts, msa_ref = refs[: g.C], refs[g.C]
    col = lax.axis_index("col")
    for k, ref in enumerate(parts):
        msa = ref[...].astype(F32).reshape(g.SP, 1, g.I, 2 * g.M)
        msa = jnp.concatenate([msa[..., : g.M], msa[..., g.M :]], axis=1)
        msa = msa.reshape(g.S, g.I, g.M)[: g.SQ].astype(BF16)
        msa_ref[pl.ds(lax.rem(col - k + g.C, g.C) * g.SQ, g.SQ)] = msa


def finish_kernel(g, msa_ref, *refs):
    parts, (out_ref, matrix_ref) = refs[: g.D], refs[g.D :]
    depth = lax.axis_index("depth")
    out_ref[...] = msa_ref[...]
    share = g.Q // g.D
    for k in range(g.D):
        first = lax.rem(depth - k + g.D, g.D) * share
        for c in range(g.C):
            block = parts[k][c].astype(F32)
            matrix_ref[pl.ds(first, share), c * g.QL : (c + 1) * g.QL, :] = block


class Sizes:
    def __init__(self, x, e, wl, w1):
        self.R, self.C, self.D = (lax.axis_size(a) for a in ("row", "col", "depth"))
        self.I, self.M = x.shape[1:]
        self.JC, self.Z = e.shape[1:]
        self.H, self.Q = wl.shape[1], w1.shape[1]
        self.QL = self.Q // self.C
        self.SQ = x.shape[0] // self.C
        self.S = -(-self.SQ // 16) * 16
        self.SP, self.N = self.S // 2, self.R * self.I
        self.F = self.R // self.C
        self.NT = -(-self.N // LANES)
        self.G = max(1, LANES // self.JC)
        self.EXTRA = -(-(self.C - 1) * self.S * self.QL // LANES)
        self.carried = 0
        self.order = [*range(self.R // 2, self.R), *range(1, self.R // 2)]

    def fill(self, rows):
        if self.SQ == self.S:
            return rows
        return rows_of([rows, jnp.zeros((self.S - self.SQ, *rows.shape[1:]), rows.dtype)])

    def place(self, row, col):
        turn = lax.rem(row // self.F - col + self.C, self.C)
        return pl.multiple_of((turn * self.F + lax.rem(row, self.F)) * self.I, self.I)


def shift(array, axis, k):
    count = lax.axis_size(axis)
    return lax.ppermute(array, axis, [(i, (i + k) % count) for i in range(count)])


def swap(array, axis, x):
    return lax.ppermute(array, axis, [(i, i ^ x) for i in range(lax.axis_size(axis))])


def swapped(arrays, axis):
    return [swap(a, axis, k + 1) for k, a in reversed([*enumerate(arrays)])]


def shifted_all(array, axis):
    return [array] + [shift(array, axis, k) for k in range(1, lax.axis_size(axis))]


def per_device(
    homolog_ensemble,
    duplex_embedding,
    homolog_present_flags,
    resolved_position_flags,
    payload_weights,
    sigmoid_weights,
    averager_final_weights,
    first_operand_weights,
    second_operand_weights,
    duplex_logit_weights,
    tensor_product_weights,
    averager_upstream_adjoint,
    duplex_upstream_adjoint,
):
    g = Sizes(homolog_ensemble, duplex_embedding, duplex_logit_weights, first_operand_weights)
    shape = jax.ShapeDtypeStruct

    def call(kernel, name, args, outs, scratch=(), far=None, after=(), distant=False, us=1.0):
        size = sum(a.size * a.dtype.itemsize for a in args) + sum(
            math.prod(o.shape) * jnp.dtype(o.dtype).itemsize for o in outs
        )
        single = len(outs) == 1
        near = len(args) if far is None else far
        args = list(args[:near]) + [
            pltpu.with_memory_space_constraint(a, pltpu.HBM) for a in args[near:]
        ]

        if distant:
            after = [pltpu.with_memory_space_constraint(a, pltpu.HBM) for a in after]

        def body(*refs):
            kernel(g, *refs[: len(args)], *refs[len(args) + len(after) :])

        return pl.pallas_call(
            body,
            out_shape=outs[0] if single else tuple(outs),
            in_specs=[VMEM] * near + [FAR] * (len(args) - near) + [FAR if distant else VMEM] * len(after),
            out_specs=VMEM if single else (VMEM,) * len(outs),
            scratch_shapes=list(scratch),
            compiler_params=pltpu.CompilerParams(vmem_limit_bytes=40 * 1024 * 1024),
            cost_estimate=pl.CostEstimate(
                flops=int(us * 1.15e9), bytes_accessed=size, transcendentals=0
            ),
            name=name,
        )(*args, *after)

    heads = g.H * g.I
    rows = g.SP * g.I
    values = 2 * payload_weights.shape[1]
    pairs, tall = g.I * g.JC, heads // g.G
    xn, send, logits, near, x, e, wl, masks, w1, outer_weights, w2 = call(
        normalise_kernel,
        "normalise",
        (
            homolog_ensemble,
            duplex_embedding,
            duplex_upstream_adjoint.reshape(pairs, g.Z),
            resolved_position_flags.reshape(1, g.JC),
            duplex_logit_weights.T,
            homolog_present_flags,
            first_operand_weights.T,
            tensor_product_weights,
            second_operand_weights.T,
        ),
        [
            pltpu.VMEM((g.C, g.SP, g.I, 2 * g.M), BF16),
            pltpu.VMEM((rows + g.EXTRA * g.I, 2 * g.M), BF16),
            pltpu.VMEM((tall, g.G * g.JC), F32),
            pltpu.VMEM((pairs + 3 * tall, g.Z), BF16),
            pltpu.VMEM((g.SQ, g.I, g.M), BF16),
            pltpu.VMEM(duplex_embedding.shape, BF16),
            pltpu.VMEM((g.H, g.Z), BF16),
            pltpu.VMEM((g.C * g.SP + 8, 2 * g.M), F32),
            pltpu.VMEM((g.Q, g.M), BF16),
            pltpu.VMEM(tensor_product_weights.shape, BF16),
            pltpu.VMEM((g.Q, g.M), BF16),
        ],
        [
            pltpu.VMEM((1, g.JC), jnp.int32),
            pltpu.SMEM(homolog_present_flags.shape, jnp.int32),
            pltpu.VMEM(homolog_ensemble.shape, BF16),
            pltpu.VMEM(homolog_ensemble.shape, F32),
            pltpu.VMEM((g.I * g.H, LANES), F32),
            pltpu.SemaphoreType.DMA((9,)),
        ],
        far=0,
        us=2.0,
    )
    everyone = [send] + [swap(send, "row", k) for k in g.order]
    nears = shifted_all(near, "col")
    later = (
        sigmoid_weights,
        averager_final_weights.T,
        payload_weights,
    )
    g.carried = len(later)
    left, weights, left_weights, u, sg, wf, p = call(
        prepare_kernel,
        "prepare",
        (xn, w1, outer_weights, masks, averager_upstream_adjoint, *later),
        [
            pltpu.VMEM((g.C * g.I * g.S, g.Q), BF16),
            pltpu.VMEM((g.Q, g.Q, g.Z), BF16),
            pltpu.VMEM((g.I, g.Q * g.S, g.Z), BF16),
            pltpu.VMEM((g.SQ, g.I, g.M), BF16),
        ]
        + [pltpu.VMEM(a.shape, a.dtype) for a in later],
        [
            pltpu.VMEM(tensor_product_weights.shape, F32),
            pltpu.VMEM((2, rows, LANES), F32),
            pltpu.SemaphoreType.DMA,
            pltpu.SemaphoreType.DMA((len(later),)),
        ],
        far=4,
        us=0.01,
    )
    gate_weights, blended, gate_factor = call(
        gate_kernel,
        "gate",
        (xn, u, sg, wf),
        [
            pltpu.VMEM((2 * g.M, values), BF16),
            pltpu.VMEM((rows, values), BF16),
            pltpu.VMEM((rows, values), F32),
        ],
        after=nears[1:],
        us=0.01,
    )
    cotangents, second_term = call(
        right_kernel,
        "right",
        (*nears, left_weights, w2, masks),
        [pltpu.VMEM((g.I, g.N, g.Z), BF16), pltpu.VMEM((g.SP, g.N, 2 * g.M), F32)],
        [pltpu.VMEM((g.NT, g.Q * g.S, LANES), F32)],
        after=(gate_weights,),
        us=0.01,
    )
    share = g.Q * g.QL // g.D
    xall, *matrix_parts = call(
        outer_kernel,
        "outer",
        (*everyone, cotangents, left, w2, masks),
        [pltpu.VMEM((g.SP, g.N, 2 * g.M), BF16)] + [pltpu.VMEM((share, g.Z), F32)] * g.D,
        [
            pltpu.VMEM((g.N, max(1, g.EXTRA) * LANES), BF16),
            pltpu.VMEM((g.NT, g.C * g.SP * 2 * g.QL, LANES), F32),
            pltpu.VMEM((g.QL * g.C * g.S, g.N), BF16),
            pltpu.VMEM((g.QL, g.C, g.I, g.S, g.Z), BF16),
            pltpu.VMEM((g.Q * g.QL, g.Z), F32),
        ],
        after=(second_term,),
        us=0.05,
    )
    matrix_parts = [matrix_parts[0]] + [
        shift(a, "depth", k + 1) for k, a in enumerate(matrix_parts[1:])
    ]
    soft, grad_soft, own, gate_grads, *sums = call(
        attend_kernel,
        "attend",
        (xall, logits, *nears[1:], blended, gate_factor, p, second_term),
        [
            pltpu.VMEM((heads, g.N), F32),
            pltpu.VMEM((heads, g.N), F32),
            pltpu.VMEM((rows, 2 * g.M), F32),
            pltpu.VMEM((rows, values), BF16),
        ]
        + [pltpu.VMEM((rows, 2 * g.M), BF16)] * (g.R - 1),
        [pltpu.VMEM((g.SP, g.N, 2 * g.M), F32)],
        us=3.0,
    )
    *sums, piece = call(
        pack_kernel,
        "pack",
        (*sums, *matrix_parts),
        [pltpu.VMEM((rows + share, 2 * g.M), BF16)] * (g.R - 1) + [pltpu.VMEM((share, g.Z), BF16)],
        us=0.2,
    )
    sums = swapped(sums, "row")
    wide = -(-3 * (g.JC + 1) // LANES) * LANES
    scores, *sends = call(
        score_kernel,
        "score",
        (soft, *shifted_all(grad_soft, "depth")),
        [pltpu.VMEM((heads, g.JC + 1), F32)] + [pltpu.VMEM((heads, wide), BF16)] * (g.C - 1),
        [pltpu.VMEM((g.D, heads, g.N), F32)],
        after=(piece,),
        us=0.2,
    )
    arrived = [shift(a, "col", k + 1) for k, a in enumerate(sends)]
    own = call(
        own_kernel,
        "own",
        (xall, cotangents, weights, w1, w2, masks, own, gate_grads, gate_weights),
        [pltpu.VMEM((rows, 2 * g.M), F32)],
        [
            pltpu.VMEM((g.NT, g.SP * 2 * g.Q, LANES), F32),
            pltpu.VMEM((g.Q * g.S, g.N), BF16),
            pltpu.VMEM((g.Q, g.I, g.S, g.Z), BF16),
            pltpu.VMEM((g.I * g.S, 2 * g.M), F32),
        ],
        after=(scores,),
        us=0.01,
    )
    piece = call(
        piece_kernel,
        "piece",
        (piece, *sums),
        [pltpu.VMEM((share, g.Z), BF16)],
        [pltpu.VMEM((g.R, share, g.Z), BF16)],
        after=(own,),
        us=0.1,
    )
    pieces = shifted_all(piece, "col")
    part = call(
        reduce_kernel,
        "reduce",
        (x, own, *sums),
        [pltpu.VMEM((rows, 2 * g.M), BF16)],
        after=(piece,),
    )
    pairwise_gradient = call(
        pair_kernel,
        "pair",
        (e, wl, soft, scores, *arrived),
        [shape(duplex_embedding.shape, BF16)],
        after=(part,),
        us=0.01,
    )
    matrix = call(
        across_kernel,
        "across",
        pieces,
        [pltpu.VMEM((g.C, share, g.Z), BF16)],
        after=(pairwise_gradient,),
        distant=True,
        us=0.1,
    ).reshape(g.C, g.Q // g.D, g.QL, g.Z)
    ensemble_derivative = call(
        unpack_kernel,
        "unpack",
        shifted_all(part, "col"),
        [pltpu.VMEM(homolog_ensemble.shape, BF16)],
        after=(matrix,),
    )
    ensemble_derivative, outer_matrix_gradient = call(
        finish_kernel,
        "finish",
        (ensemble_derivative, *shifted_all(matrix, "depth")),
        [shape(homolog_ensemble.shape, BF16), shape((g.Q, g.Q, g.Z), F32)],
    )
    outer_matrix_gradient = outer_matrix_gradient.reshape(tensor_product_weights.shape)
    return (ensemble_derivative, pairwise_gradient, outer_matrix_gradient)


def solution(mesh):
    in_specs = (
        P(("parts", "depth"), "row", None),
        P(("parts", "row"), "col", None),
        P("parts"),
        P(("parts", "col")),
        P(),
        P(),
        P(),
        P(),
        P(),
        P(),
        P(),
        P(("parts", "depth"), "row", None),
        P(("parts", "row"), "col", None),
    )
    out_specs = (
        P(("parts", "depth"), "row", None),
        P(("parts", "row"), "col", None),
        P("parts", None),
    )
    return jax.shard_map(
        per_device, mesh=mesh, in_specs=in_specs, out_specs=out_specs, check_vma=False
    )
```

profile of v0, /device:TPU:0, one launch (start us, length us, event | category | flops | bytes accessed | tf_op | source)
XLA Modules:
  0.0 36.8 jit_solution(6365732856413033500)
XLA Ops:
  0.6 2.1 %normalise.1 = (bf16[2,8,16,128]{3,2,1,0:T(8,128)(2,1)S(1)}, bf16[160,128]{1,0:T(8,128)(2,1)S(1)}, f32[32,128]{1,0:T(8,128)S(1)}, bf16[608,128]{1,0:T(8,128)(2,1...) custom-call(bf16[32,16,64]{2,1,0:T(8,128)(2,1)} %refs_0_.1, ...), custom_call_target="tpu_custom_call" | custom-call | flops 2300000000 | bytes 1327488 | tf_op jit(solution)/shard_map/normalise/pallas_call | solution.py:628
  2.8 3.0 %collective-permute-start.3 = (bf16[608,128]{1,0:T(8,128)(2,1)S(1)}, bf16[608,128]{1,0:T(8,128)(2,1)S(1)}, u32[]{:S(2)}, u32[]{:S(2)}) collective-permute-start(bf16[608,128]{1,0:T(8,128)(2,1)S(1)} %get-tuple-element.46.refs_0_), channel_id=1, source_target_pairs={{0,2},{2,0},{1,3},{3,1},{4,6},{6,4},{5,7},{7,5},{8,10},{10,8},{9,1... | collective-permute-start | bytes 466952 | tf_op jit(solution)/shard_map/ppermute | solution.py:579
  5.8 2.6 %collective-permute-start = (bf16[160,128]{1,0:T(8,128)(2,1)S(1)}, bf16[160,128]{1,0:T(8,128)(2,1)S(1)}, u32[]{:S(2)}, u32[]{:S(2)}) collective-permute-start(bf16[160,128]{1,0:T(8,128)(2,1)S(1)} %get-tuple-element.45.refs_0_), channel_id=1, source_target_pairs={{0,8},{4,12},{8,0},{12,4},{1,9},{5,13},{9,1},{13,5},{2,10},{6,14},... | collective-permute-start | bytes 122888 | tf_op jit(solution)/shard_map/ppermute | solution.py:583
  8.4 1.3 %collective-permute-start.1 = (bf16[160,128]{1,0:T(8,128)(2,1)S(1)}, bf16[160,128]{1,0:T(8,128)(2,1)S(1)}, u32[]{:S(2)}, u32[]{:S(2)}) collective-permute-start(bf16[160,128]{1,0:T(8,128)(2,1)S(1)} %get-tuple-element.45.refs_0_), channel_id=1, source_target_pairs={{0,12},{4,8},{8,4},{12,0},{1,13},{5,9},{9,5},{13,1},{2,14},{6,10},... | collective-permute-start | bytes 122888 | tf_op jit(solution)/shard_map/ppermute | solution.py:583
  9.7 0.2 collective-permute-start.2
  9.9 1.5 %prepare.1 = (bf16[512,32]{1,0:T(8,128)(2,1)S(1)}, bf16[32,32,128]{2,1,0:T(8,128)(2,1)S(1)}, bf16[16,512,128]{2,1,0:T(8,128)(2,1)S(1)}, bf16[16,16,64]{2,1,0:T(8...) custom-call(bf16[2,8,16,128]{3,2,1,0:T(8,128)(2,1)S(1)} %get-tuple-element.47., ...), custom_call_target="tpu_custom_call" | custom-call | flops 11500000 | bytes 3031040 | tf_op jit(solution)/shard_map/prepare/pallas_call | solution.py:628
  11.4 0.0 collective-permute-done.3.refs_4_.refs_1_.refs_2_
  11.5 0.2 gate.1
  11.7 1.1 %right.1 = (bf16[16,64,128]{2,1,0:T(8,128)(2,1)S(1)}, f32[8,64,128]{2,1,0:T(8,128)S(1)}) custom-call(bf16[608,128]{1,0:T(8,128)(2,1)S(1)} %get-tuple-element.46.refs_0_, bf16[608,128]{1,0:T(8,128)(2,1)S(1)} %collective-permute-done.3.refs_4_.refs_1_.refs_2_, bf16[16,512,128]{2,1,0:T(8,128)(2,1)S(1)} %get-tuple-element.51.refs_2_, ...), custom_call_target="tpu_custom_call" | custom-call | flops 11500000 | bytes 2949120 | tf_op jit(solution)/shard_map/right/pallas_call | solution.py:628
  12.8 0.0 collective-permute-done.refs_1_
  12.8 1.3 %collective-permute-done.1.refs_2_ = bf16[160,128]{1,0:T(8,128)(2,1)S(1)} collective-permute-done((bf16[160,128]{1,0:T(8,128)(2,1)S(1)}, bf16[160,128]{1,0:T(8,128)(2,1)S(1)}, u32[]{:S(2)}, u32[]{:S(2)}) %collective-permute-start.1) | collective-permute-done | bytes 40992 | tf_op jit(solution)/shard_map/ppermute | solution.py:583
  14.2 1.6 %outer.1 = (bf16[8,64,128]{2,1,0:T(8,128)(2,1)S(1)}, f32[256,128]{1,0:T(8,128)S(1)}, f32[256,128]{1,0:T(8,128)S(1)}) custom-call(bf16[160,128]{1,0:T(8,128)(2,1)S(1)} %get-tuple-element.45.refs_0_, bf16[160,128]{1,0:T(8,128)(2,1)S(1)} %collective-permute-done.refs_1_, bf16[160,128]{1,0:T(8,128)(2,1)S(1)} %collective-permute-done.1.refs_2_, ...), custom_call_target="tpu_custom_call" | custom-call | flops 57500000 | bytes 868352 | tf_op jit(solution)/shard_map/outer/pallas_call | solution.py:628
  15.8 0.1 collective-permute-start.5
  15.9 2.5 %attend.1 = (f32[128,64]{1,0:T(8,128)S(1)}, f32[128,64]{1,0:T(8,128)S(1)}, f32[128,128]{1,0:T(8,128)S(1)}, bf16[128,512]{1,0:T(8,128)(2,1)S(1)}, bf16[128,128]{1...) custom-call(bf16[8,64,128]{2,1,0:T(8,128)(2,1)S(1)} %get-tuple-element.60.refs_0_, ...), custom_call_target="tpu_custom_call" | custom-call | flops 3449999872 | bytes 1351680 | tf_op jit(solution)/shard_map/attend/pallas_call | solution.py:628
  18.5 2.1 %collective-permute-start.6 = (bf16[384,128]{1,0:T(8,128)(2,1)S(1)}, bf16[384,128]{1,0:T(8,128)(2,1)S(1)}, u32[]{:S(2)}, u32[]{:S(2)}) collective-permute-start(bf16[384,128]{1,0:T(8,128)(2,1)S(1)} %get-tuple-element.77), channel_id=1, source_target_pairs={{0,12},{4,8},{8,4},{12,0},{1,13},{5,9},{9,5},{13,1},{2,14},{6,10},... | collective-permute-start | bytes 294920 | tf_op jit(solution)/shard_map/ppermute | solution.py:583
  20.6 2.4 %collective-permute-start.8 = (bf16[384,128]{1,0:T(8,128)(2,1)S(1)}, bf16[384,128]{1,0:T(8,128)(2,1)S(1)}, u32[]{:S(2)}, u32[]{:S(2)}) collective-permute-start(bf16[384,128]{1,0:T(8,128)(2,1)S(1)} %get-tuple-element.79), channel_id=1, source_target_pairs={{0,4},{4,0},{8,12},{12,8},{1,5},{5,1},{9,13},{13,9},{2,6},{6,2},{1... | collective-permute-start | bytes 294920 | tf_op jit(solution)/shard_map/ppermute | solution.py:583
  22.9 1.3 %collective-permute-done.4.refs_2_ = f32[128,64]{1,0:T(8,128)S(1)} collective-permute-done((f32[128,64]{1,0:T(8,128)S(1)}, f32[128,64]{1,0:T(8,128)S(1)}, u32[]{:S(2)}, u32[]{:S(2)}) %collective-permute-start.4) | collective-permute-done | bytes 32800 | tf_op jit(solution)/shard_map/ppermute | solution.py:579
  24.2 0.2 score.1
  24.4 0.6 %collective-permute-start.11 = (bf16[128,128]{1,0:T(8,128)(2,1)S(1)}, bf16[128,128]{1,0:T(8,128)(2,1)S(1)}, u32[]{:S(2)}, u32[]{:S(2)}) collective-permute-start(bf16[128,128]{1,0:T(8,128)(2,1)S(1)} %get-tuple-element.82), channel_id=1, source_target_pairs={{0,2},{2,0},{1,3},{3,1},{4,6},{6,4},{5,7},{7,5},{8,10},{10,8},{9,1... | collective-permute-start | bytes 98312 | tf_op jit(solution)/shard_map/ppermute | solution.py:579
  25.0 2.8 %own.1.refs_4_.refs_1_ = f32[128,128]{1,0:T(8,128)S(1)} custom-call(bf16[8,64,128]{2,1,0:T(8,128)(2,1)S(1)} %get-tuple-element.60.refs_0_, bf16[16,64,128]{2,1,0:T(8,128)(2,1)S(1)} %get-tuple-element.57.refs_4_.refs_1_, bf16[32,32,128]{2,1,0:T(8,128)(2,1)S(1)} %get-tuple-element.61.refs_2_, bf16[32,64]{1,0:T(8,128)(2,1)S(1)} %get-tuple-element.48.refs_1_.refs_3_, ...), custom_call_target="tpu_custom_call" | custom-call | flops 11500000 | bytes 1069056 | tf_op jit(solution)/shard_map/own/pallas_call | solution.py:628
  27.8 2.2 %collective-permute-done.7.refs_2_.refs_3_ = bf16[384,128]{1,0:T(8,128)(2,1)S(1)} collective-permute-done((bf16[384,128]{1,0:T(8,128)(2,1)S(1)}, bf16[384,128]{1,0:T(8,128)(2,1)S(1)}, u32[]{:S(2)}, u32[]{:S(2)}) %collective-permute-start.7) | collective-permute-done | bytes 98336 | tf_op jit(solution)/shard_map/ppermute | solution.py:583
  30.0 0.1 piece.1.refs_5_.refs_0_
  30.0 0.6 %collective-permute-start.10 = (bf16[256,128]{1,0:T(8,128)(2,1)S(1)}, bf16[256,128]{1,0:T(8,128)(2,1)S(1)}, u32[]{:S(2)}, u32[]{:S(2)}) collective-permute-start(bf16[256,128]{1,0:T(8,128)(2,1)S(1)} %piece.1.refs_5_.refs_0_), channel_id=1, source_target_pairs={{0,2},{2,0},{1,3},{3,1},{4,6},{6,4},{5,7},{7,5},{8,10},{10,8},{9,1... | collective-permute-start | bytes 196616 | tf_op jit(solution)/shard_map/ppermute | solution.py:579
  30.7 0.4 reduce.1.refs_5_.refs_0_
  31.0 1.5 %collective-permute-start.9 = (bf16[128,128]{1,0:T(8,128)(2,1)S(1)}, bf16[128,128]{1,0:T(8,128)(2,1)S(1)}, u32[]{:S(2)}, u32[]{:S(2)}) collective-permute-start(bf16[128,128]{1,0:T(8,128)(2,1)S(1)} %reduce.1.refs_5_.refs_0_), channel_id=1, source_target_pairs={{0,2},{2,0},{1,3},{3,1},{4,6},{6,4},{5,7},{7,5},{8,10},{10,8},{9,1... | collective-permute-start | bytes 98312 | tf_op jit(solution)/shard_map/ppermute | solution.py:579
  32.6 1.7 %pair.1.refs_2_ = bf16[16,32,128]{2,1,0:T(8,128)(2,1)} custom-call(bf16[16,32,128]{2,1,0:T(8,128)(2,1)S(1)} %get-tuple-element.80.refs_0_, bf16[8,128]{1,0:T(8,128)(2,1)S(1)} %get-tuple-element.81.refs_1_, f32[128,64]{1,0:T(8,128)S(1)} %get-tuple-element.68.refs_0_.refs_2_, f32[128,33]{1,0:T(8,128)S(1)} %get-tuple-element.76.refs_9_.refs_3_, ...), custom_call_target="tpu_custom_call" | custom-call | flops 11500000 | bytes 346624 | tf_op jit(solution)/shard_map/pair/pallas_call | solution.py:628
  34.3 0.2 collective-permute-done.10.refs_1_
  34.5 0.1 collective-permute-start.12
  34.6 0.4 %collective-permute-done.9.refs_1_ = bf16[128,128]{1,0:T(8,128)(2,1)S(1)} collective-permute-done((bf16[128,128]{1,0:T(8,128)(2,1)S(1)}, bf16[128,128]{1,0:T(8,128)(2,1)S(1)}, u32[]{:S(2)}, u32[]{:S(2)}) %collective-permute-start.9) | collective-permute-done | bytes 32800 | tf_op jit(solution)/shard_map/ppermute | solution.py:579
  35.0 0.1 unpack.1.refs_0_
  35.1 0.8 %collective-permute-done.12.refs_2_ = bf16[2,16,16,128]{3,2,1,0:T(8,128)(2,1)S(1)} collective-permute-done((bf16[2,16,16,128]{3,2,1,0:T(8,128)(2,1)S(1)}, bf16[2,16,16,128]{3,2,1,0:T(8,128)(2,1)S(1)}, u32[]{:S(2)}, u32[]{:S(2)}) %collective-permute-start.12) | collective-permute-done | bytes 131104 | tf_op jit(solution)/shard_map/ppermute | solution.py:579
  35.9 0.9 %finish.1 = (bf16[32,16,64]{2,1,0:T(8,128)(2,1)}, f32[32,32,128]{2,1,0:T(8,128)}) custom-call(bf16[32,16,64]{2,1,0:T(8,128)(2,1)S(1)} %unpack.1.refs_0_, bf16[2,16,16,128]{3,2,1,0:T(8,128)(2,1)S(1)} %bitcast.10, bf16[2,16,16,128]{3,2,1,0:T(8,128)(2,1)S(1)} %collective-permute-done.12.refs_2_), custom_call_target="tpu_custom_call" | custom-call | flops 1150000000 | bytes 917504 | tf_op jit(solution)/shard_map/finish/pallas_call | solution.py:628
  (9 shorter events, 0.1 us)
Async XLA Ops:
  2.8 8.7 %collective-permute-start.3 = (bf16[608,128]{1,0:T(8,128)(2,1)S(1)}, bf16[608,128]{1,0:T(8,128)(2,1)S(1)}, u32[]{:S(2)}, u32[]{:S(2)}) collective-permute-start(bf16[608,128]{1,0:T(8,128)(2,1)S(1)} %get-tuple-element.46.refs_0_), channel_id=1, source_target_pairs={{0,2},{2,0},{1,3},{3,1},{4,6},{6,4},{5,7},{7,5},{8,10},{10,8},{9,1... | collective-permute-start | bytes 466952 | tf_op jit(solution)/shard_map/ppermute | solution.py:579
  5.8 7.0 %collective-permute-start = (bf16[160,128]{1,0:T(8,128)(2,1)S(1)}, bf16[160,128]{1,0:T(8,128)(2,1)S(1)}, u32[]{:S(2)}, u32[]{:S(2)}) collective-permute-start(bf16[160,128]{1,0:T(8,128)(2,1)S(1)} %get-tuple-element.45.refs_0_), channel_id=1, source_target_pairs={{0,8},{4,12},{8,0},{12,4},{1,9},{5,13},{9,1},{13,5},{2,10},{6,14},... | collective-permute-start | bytes 122888 | tf_op jit(solution)/shard_map/ppermute | solution.py:583
  8.4 5.8 %collective-permute-start.1 = (bf16[160,128]{1,0:T(8,128)(2,1)S(1)}, bf16[160,128]{1,0:T(8,128)(2,1)S(1)}, u32[]{:S(2)}, u32[]{:S(2)}) collective-permute-start(bf16[160,128]{1,0:T(8,128)(2,1)S(1)} %get-tuple-element.45.refs_0_), channel_id=1, source_target_pairs={{0,12},{4,8},{8,4},{12,0},{1,13},{5,9},{9,5},{13,1},{2,14},{6,10},... | collective-permute-start | bytes 122888 | tf_op jit(solution)/shard_map/ppermute | solution.py:583
  9.7 4.5 %collective-permute-start.2 = (bf16[160,128]{1,0:T(8,128)(2,1)S(1)}, bf16[160,128]{1,0:T(8,128)(2,1)S(1)}, u32[]{:S(2)}, u32[]{:S(2)}) collective-permute-start(bf16[160,128]{1,0:T(8,128)(2,1)S(1)} %get-tuple-element.45.refs_0_), channel_id=1, source_target_pairs={{0,4},{4,0},{8,12},{12,8},{1,5},{5,1},{9,13},{13,9},{2,6},{6,2},{1... | collective-permute-start | bytes 122888 | tf_op jit(solution)/shard_map/ppermute | solution.py:583
  15.8 2.6 %collective-permute-start.5 = (f32[256,128]{1,0:T(8,128)S(1)}, f32[256,128]{1,0:T(8,128)S(1)}, u32[]{:S(2)}, u32[]{:S(2)}) collective-permute-start(f32[256,128]{1,0:T(8,128)S(1)} %get-tuple-element.74), channel_id=1, source_target_pairs={{0,1},{1,0},{2,3},{3,2},{4,5},{5,4},{6,7},{7,6},{8,9},{9,8},{10,11... | collective-permute-start | bytes 393224 | tf_op jit(solution)/shard_map/ppermute | solution.py:579
  18.5 9.3 %collective-permute-start.6 = (bf16[384,128]{1,0:T(8,128)(2,1)S(1)}, bf16[384,128]{1,0:T(8,128)(2,1)S(1)}, u32[]{:S(2)}, u32[]{:S(2)}) collective-permute-start(bf16[384,128]{1,0:T(8,128)(2,1)S(1)} %get-tuple-element.77), channel_id=1, source_target_pairs={{0,12},{4,8},{8,4},{12,0},{1,13},{5,9},{9,5},{13,1},{2,14},{6,10},... | collective-permute-start | bytes 294920 | tf_op jit(solution)/shard_map/ppermute | solution.py:583
  20.6 9.4 %collective-permute-start.7 = (bf16[384,128]{1,0:T(8,128)(2,1)S(1)}, bf16[384,128]{1,0:T(8,128)(2,1)S(1)}, u32[]{:S(2)}, u32[]{:S(2)}) collective-permute-start(bf16[384,128]{1,0:T(8,128)(2,1)S(1)} %get-tuple-element.78), channel_id=1, source_target_pairs={{0,8},{4,12},{8,0},{12,4},{1,9},{5,13},{9,1},{13,5},{2,10},{6,14},... | collective-permute-start | bytes 294920 | tf_op jit(solution)/shard_map/ppermute | solution.py:583
  20.6 9.4 %collective-permute-start.8 = (bf16[384,128]{1,0:T(8,128)(2,1)S(1)}, bf16[384,128]{1,0:T(8,128)(2,1)S(1)}, u32[]{:S(2)}, u32[]{:S(2)}) collective-permute-start(bf16[384,128]{1,0:T(8,128)(2,1)S(1)} %get-tuple-element.79), channel_id=1, source_target_pairs={{0,4},{4,0},{8,12},{12,8},{1,5},{5,1},{9,13},{13,9},{2,6},{6,2},{1... | collective-permute-start | bytes 294920 | tf_op jit(solution)/shard_map/ppermute | solution.py:583
  22.9 1.3 %collective-permute-start.4 = (f32[128,64]{1,0:T(8,128)S(1)}, f32[128,64]{1,0:T(8,128)S(1)}, u32[]{:S(2)}, u32[]{:S(2)}) collective-permute-start(f32[128,64]{1,0:T(8,128)S(1)} %get-tuple-element.69.refs_1_), channel_id=1, source_target_pairs={{0,1},{1,0},{2,3},{3,2},{4,5},{5,4},{6,7},{7,6},{8,9},{9,8},{10,11... | collective-permute-start | bytes 98312 | tf_op jit(solution)/shard_map/ppermute | solution.py:579
  24.4 8.2 %collective-permute-start.11 = (bf16[128,128]{1,0:T(8,128)(2,1)S(1)}, bf16[128,128]{1,0:T(8,128)(2,1)S(1)}, u32[]{:S(2)}, u32[]{:S(2)}) collective-permute-start(bf16[128,128]{1,0:T(8,128)(2,1)S(1)} %get-tuple-element.82), channel_id=1, source_target_pairs={{0,2},{2,0},{1,3},{3,1},{4,6},{6,4},{5,7},{7,5},{8,10},{10,8},{9,1... | collective-permute-start | bytes 98312 | tf_op jit(solution)/shard_map/ppermute | solution.py:579
  30.0 4.5 %collective-permute-start.10 = (bf16[256,128]{1,0:T(8,128)(2,1)S(1)}, bf16[256,128]{1,0:T(8,128)(2,1)S(1)}, u32[]{:S(2)}, u32[]{:S(2)}) collective-permute-start(bf16[256,128]{1,0:T(8,128)(2,1)S(1)} %piece.1.refs_5_.refs_0_), channel_id=1, source_target_pairs={{0,2},{2,0},{1,3},{3,1},{4,6},{6,4},{5,7},{7,5},{8,10},{10,8},{9,1... | collective-permute-start | bytes 196616 | tf_op jit(solution)/shard_map/ppermute | solution.py:579
  31.0 4.0 %collective-permute-start.9 = (bf16[128,128]{1,0:T(8,128)(2,1)S(1)}, bf16[128,128]{1,0:T(8,128)(2,1)S(1)}, u32[]{:S(2)}, u32[]{:S(2)}) collective-permute-start(bf16[128,128]{1,0:T(8,128)(2,1)S(1)} %reduce.1.refs_5_.refs_0_), channel_id=1, source_target_pairs={{0,2},{2,0},{1,3},{3,1},{4,6},{6,4},{5,7},{7,5},{8,10},{10,8},{9,1... | collective-permute-start | bytes 98312 | tf_op jit(solution)/shard_map/ppermute | solution.py:579
  34.5 1.4 %collective-permute-start.12 = (bf16[2,16,16,128]{3,2,1,0:T(8,128)(2,1)S(1)}, bf16[2,16,16,128]{3,2,1,0:T(8,128)(2,1)S(1)}, u32[]{:S(2)}, u32[]{:S(2)}) collective-permute-start(bf16[2,16,16,128]{3,2,1,0:T(8,128)(2,1)S(1)} %bitcast.8), channel_id=1, source_target_pairs={{0,1},{1,0},{2,3},{3,2},{4,5},{5,4},{6,7},{7,6},{8,9},{9,8},{10,11... | collective-permute-start | bytes 393224 | tf_op jit(solution)/shard_map/ppermute | solution.py:579
where the time goes:
time: 37 us; the launch traced here: 36.8 us
  Pallas kernels  15.3 us (41%)
  starting transfers between devices  14.5 us (39%)
  waiting for transfers between devices  6.22 us (17%)
  between operations  0.78 us (2%)
    pallas_call x15, Pallas kernels, call(): pl.pallas_call(body, out_shape=outs[0] if single else tuple(outs), in_spe...  15.3 us
    ppermute x6, starting transfers between devices, swap(): lax.ppermute(array, axis, [(i, i ^ x) for i in range(lax.axis_size(axis))])  8.62 us
    ppermute x7, starting transfers between devices, shift(): lax.ppermute(array, axis, [(i, (i + k) % count) for i in range(count)])  5.9 us
    ppermute x6, waiting for transfers between devices, swap(): lax.ppermute(array, axis, [(i, i ^ x) for i in range(lax.axis_size(axis))])  3.51 us
    ppermute x7, waiting for transfers between devices, shift(): lax.ppermute(array, axis, [(i, (i + k) % count) for i in range(count)])  2.71 us
  transfers between devices with their start and end apart: 13, of which 6 were waited for; matrix products, arithmetic and copies ran while one was open for 0% of the time, Pallas kernels for 29%

commit v1 on v0

--- a/solution.py
+++ b/solution.py
@@ -89,10 +89,10 @@
 
 
 def normalise_kernel(
-    g, x_hbm, e_hbm, dd_hbm, flag_hbm, wl_hbm, live_hbm, w1_hbm, t_hbm, w2_hbm, *refs
+    g, x_hbm, e_hbm, dd_hbm, flag_hbm, wl_hbm, live_hbm, w1_hbm, t_hbm, w2_hbm, every_hbm, *refs
 ):
     xn_ref, send_ref, logit_ref, near_ref, x_ref, e_ref, wl_ref, mask_ref, w1_ref, t_ref, w2_ref = refs[:11]
-    flag_in, live_in, x_in, norm_ref, rows_ref, sem = refs[11:]
+    flag_in, live_in, every_in, x_in, norm_ref, rows_ref, sem = refs[11:]
     col = lax.axis_index("col")
     pairs = g.I * g.JC
     copies = [
@@ -108,6 +108,7 @@
                 (w1_hbm, w1_ref),
                 (t_hbm, t_ref),
                 (w2_hbm, w2_ref),
+                (every_hbm, every_in),
             ]
         )
     ]
@@ -125,11 +126,9 @@
             else:
                 flags = jnp.zeros((1, 2 * g.M), F32)
             mask_ref[m * g.SP + k : m * g.SP + k + 1, :] = flags
-    total = live_in[0]
-    for k in range(1, live_in.shape[0]):
-        total = total + live_in[k]
-    count = jnp.full((1, 2 * g.M), total, jnp.int32).astype(F32)
-    mask_ref[g.C * g.SP : g.C * g.SP + 1, :] = 1.0 / (0.001 + count)
+    copies[9].wait()
+    count = jnp.sum(every_in[...].astype(F32), -1, keepdims=True)
+    mask_ref[g.C * g.SP : g.C * g.SP + 1, :] = jnp.broadcast_to(1.0 / (0.001 + count), (1, 2 * g.M))
     copies[0].wait()
     copies[8].wait()
     norm_ref[...] = standardize(x_in[...].astype(F32))[0]
@@ -405,27 +404,40 @@
     low_t = mm(eye, low, NT).astype(BF16)
     value_weights = twice(p_ref[...])
     values = mm(xall_ref[...].reshape(g.SP * g.N, 2 * g.M), value_weights).astype(BF16)
-    wide = value_weights.shape[1]
-    head = iota((1, wide), 1) % (wide // 2) // (wide // 2 // g.H)
-    grad_soft = jnp.zeros((g.H * g.I, g.N), F32)
+    half = value_weights.shape[1] // 2
+    width = half // g.H
+    group = LANES // width
+    count = g.H // group
+    tall = group * g.I
+    head = iota((1, 2 * LANES), 1) % LANES // width
+
+    def lanes(array, k):
+        return lanes_of([array[:, s * half + k * LANES : s * half + (k + 1) * LANES] for s in range(2)])
+
+    group_weights = [lanes(value_weights, k) for k in range(count)]
+    low_t = lanes_of([low_t, low_t])
+    grad_soft = [jnp.zeros((tall, g.N), F32) for _ in range(count)]
     for k in range(g.SP):
         v = values[k * g.N : (k + 1) * g.N]
-        crossed = mm(low, v)
-        mixed = jnp.where(head == 0, crossed[: g.I], 0.0)
-        for h in range(1, g.H):
-            mixed = jnp.where(head == h, crossed[h * g.I : (h + 1) * g.I], mixed)
         rows = slice(k * g.I, (k + 1) * g.I)
-        gg_ref[rows, :] = (gate_ref[rows, :] * mixed).astype(BF16)
-        blended = gm_ref[rows, :]
-        by_head = rows_of(
-            [jnp.where(head == h, blended, jnp.zeros_like(blended)) for h in range(g.H)]
-        )
-        grad_soft = grad_soft + mm(by_head, v, NT)
-        part = go_ref[k]
-        for piece in split_high_low(mm(low_t, by_head)):
-            part = part + mm(piece, value_weights, NT)
-        total_ref[k] = part
-    gs_ref[...] = grad_soft
+        blended, factor = gm_ref[rows, :], gate_ref[rows, :]
+        projected = []
+        for m in range(count):
+            vm = lanes(v, m)
+            crossed = mm(low[m * tall : (m + 1) * tall], vm)
+            mixed = crossed[: g.I]
+            for h in range(1, group):
+                mixed = jnp.where(head == h, crossed[h * g.I : (h + 1) * g.I], mixed)
+            gate_grad = (lanes(factor, m) * mixed).astype(BF16)
+            for s in range(2):
+                first = s * half + m * LANES
+                gg_ref[rows, first : first + LANES] = gate_grad[:, s * LANES : (s + 1) * LANES]
+            bm = lanes(blended, m)
+            by_head = rows_of([jnp.where(head == h, bm, jnp.zeros_like(bm)) for h in range(group)])
+            grad_soft[m] = grad_soft[m] + mm(by_head, vm, NT)
+            projected.append(mm(by_head, group_weights[m], NT))
+        total_ref[k] = go_ref[k] + mm(low_t, rows_of([*split_high_low(rows_of(projected))]))
+    gs_ref[...] = rows_of(grad_soft)
     own = total_ref[:, pl.ds(g.place(row, col), g.I), :]
     own_ref[...] = own.reshape(g.SP * g.I, 2 * g.M)
     for x in range(1, g.R):
@@ -655,6 +667,7 @@
             first_operand_weights.T,
             tensor_product_weights,
             second_operand_weights.T,
+            homolog_present_flags.reshape(1, -1),
         ),
         [
             pltpu.VMEM((g.C, g.SP, g.I, 2 * g.M), BF16),
@@ -672,10 +685,11 @@
         [
             pltpu.VMEM((1, g.JC), jnp.int32),
             pltpu.SMEM(homolog_present_flags.shape, jnp.int32),
+            pltpu.VMEM((1, homolog_present_flags.shape[0]), jnp.int32),
             pltpu.VMEM(homolog_ensemble.shape, BF16),
             pltpu.VMEM(homolog_ensemble.shape, F32),
             pltpu.VMEM((g.I * g.H, LANES), F32),
-            pltpu.SemaphoreType.DMA((9,)),
+            pltpu.SemaphoreType.DMA((10,)),
         ],
         far=0,
         us=2.0,

time: 37 us -> 36.7 us (level)
  transfers between devices with their start and end apart: 13 -> 13, of which waited for: 6 -> 6; matrix products, arithmetic and copies ran while one was open for 0% -> 0% of each run, Pallas kernels for 29% -> 28%
where the time goes in v1:
time: 36.7 us; the launch traced here: 36.5 us
  Pallas kernels  15 us (41%)
  starting transfers between devices  14.5 us (40%)
  waiting for transfers between devices  6.21 us (17%)
  between operations  0.78 us (2%)
    pallas_call x15, Pallas kernels, call(): pl.pallas_call(body, out_shape=outs[0] if single else tuple(outs), in_spe...  15 us
    ppermute x6, starting transfers between devices, swap(): lax.ppermute(array, axis, [(i, i ^ x) for i in range(lax.axis_size(axis))])  8.62 us
    ppermute x7, starting transfers between devices, shift(): lax.ppermute(array, axis, [(i, (i + k) % count) for i in range(count)])  5.91 us
    ppermute x6, waiting for transfers between devices, swap(): lax.ppermute(array, axis, [(i, i ^ x) for i in range(lax.axis_size(axis))])  3.52 us
    ppermute x7, waiting for transfers between devices, shift(): lax.ppermute(array, axis, [(i, (i + k) % count) for i in range(count)])  2.69 us
  transfers between devices with their start and end apart: 13, of which 6 were waited for; matrix products, arithmetic and copies ran while one was open for 0% of the time, Pallas kernels for 28%

profile of v1, /device:TPU:0, one launch (start us, length us, event | category | flops | bytes accessed | tf_op | source)
XLA Modules:
  0.0 36.5 jit_solution(4318066980146520383)
XLA Ops:
  0.6 2.2 %normalise.1 = (bf16[2,8,16,128]{3,2,1,0:T(8,128)(2,1)S(1)}, bf16[160,128]{1,0:T(8,128)(2,1)S(1)}, f32[32,128]{1,0:T(8,128)S(1)}, bf16[608,128]{1,0:T(8,128)(2,1...) custom-call(bf16[32,16,64]{2,1,0:T(8,128)(2,1)} %refs_0_.1, ...), custom_call_target="tpu_custom_call" | custom-call | flops 2300000000 | bytes 1327744 | tf_op jit(solution)/shard_map/normalise/pallas_call | solution.py:640
  2.8 3.0 %collective-permute-start.3 = (bf16[608,128]{1,0:T(8,128)(2,1)S(1)}, bf16[608,128]{1,0:T(8,128)(2,1)S(1)}, u32[]{:S(2)}, u32[]{:S(2)}) collective-permute-start(bf16[608,128]{1,0:T(8,128)(2,1)S(1)} %get-tuple-element.46.refs_0_), channel_id=1, source_target_pairs={{0,2},{2,0},{1,3},{3,1},{4,6},{6,4},{5,7},{7,5},{8,10},{10,8},{9,1... | collective-permute-start | bytes 466952 | tf_op jit(solution)/shard_map/ppermute | solution.py:591
  5.8 2.6 %collective-permute-start = (bf16[160,128]{1,0:T(8,128)(2,1)S(1)}, bf16[160,128]{1,0:T(8,128)(2,1)S(1)}, u32[]{:S(2)}, u32[]{:S(2)}) collective-permute-start(bf16[160,128]{1,0:T(8,128)(2,1)S(1)} %get-tuple-element.45.refs_0_), channel_id=1, source_target_pairs={{0,8},{4,12},{8,0},{12,4},{1,9},{5,13},{9,1},{13,5},{2,10},{6,14},... | collective-permute-start | bytes 122888 | tf_op jit(solution)/shard_map/ppermute | solution.py:595
  8.4 1.3 %collective-permute-start.1 = (bf16[160,128]{1,0:T(8,128)(2,1)S(1)}, bf16[160,128]{1,0:T(8,128)(2,1)S(1)}, u32[]{:S(2)}, u32[]{:S(2)}) collective-permute-start(bf16[160,128]{1,0:T(8,128)(2,1)S(1)} %get-tuple-element.45.refs_0_), channel_id=1, source_target_pairs={{0,12},{4,8},{8,4},{12,0},{1,13},{5,9},{9,5},{13,1},{2,14},{6,10},... | collective-permute-start | bytes 122888 | tf_op jit(solution)/shard_map/ppermute | solution.py:595
  9.8 0.2 collective-permute-start.2
  10.0 1.5 %prepare.1 = (bf16[512,32]{1,0:T(8,128)(2,1)S(1)}, bf16[32,32,128]{2,1,0:T(8,128)(2,1)S(1)}, bf16[16,512,128]{2,1,0:T(8,128)(2,1)S(1)}, bf16[16,16,64]{2,1,0:T(8...) custom-call(bf16[2,8,16,128]{3,2,1,0:T(8,128)(2,1)S(1)} %get-tuple-element.47., ...), custom_call_target="tpu_custom_call" | custom-call | flops 11500000 | bytes 3031040 | tf_op jit(solution)/shard_map/prepare/pallas_call | solution.py:640
  11.5 0.0 collective-permute-done.3.refs_4_.refs_1_.refs_2_
  11.5 0.2 gate.1
  11.8 1.1 %right.1 = (bf16[16,64,128]{2,1,0:T(8,128)(2,1)S(1)}, f32[8,64,128]{2,1,0:T(8,128)S(1)}) custom-call(bf16[608,128]{1,0:T(8,128)(2,1)S(1)} %get-tuple-element.46.refs_0_, bf16[608,128]{1,0:T(8,128)(2,1)S(1)} %collective-permute-done.3.refs_4_.refs_1_.refs_2_, bf16[16,512,128]{2,1,0:T(8,128)(2,1)S(1)} %get-tuple-element.51.refs_2_, ...), custom_call_target="tpu_custom_call" | custom-call | flops 11500000 | bytes 2949120 | tf_op jit(solution)/shard_map/right/pallas_call | solution.py:640
  12.9 1.3 %collective-permute-done.1.refs_2_ = bf16[160,128]{1,0:T(8,128)(2,1)S(1)} collective-permute-done((bf16[160,128]{1,0:T(8,128)(2,1)S(1)}, bf16[160,128]{1,0:T(8,128)(2,1)S(1)}, u32[]{:S(2)}, u32[]{:S(2)}) %collective-permute-start.1) | collective-permute-done | bytes 40992 | tf_op jit(solution)/shard_map/ppermute | solution.py:595
  14.2 1.6 %outer.1 = (bf16[8,64,128]{2,1,0:T(8,128)(2,1)S(1)}, f32[256,128]{1,0:T(8,128)S(1)}, f32[256,128]{1,0:T(8,128)S(1)}) custom-call(bf16[160,128]{1,0:T(8,128)(2,1)S(1)} %get-tuple-element.45.refs_0_, bf16[160,128]{1,0:T(8,128)(2,1)S(1)} %collective-permute-done.refs_1_, bf16[160,128]{1,0:T(8,128)(2,1)S(1)} %collective-permute-done.1.refs_2_, ...), custom_call_target="tpu_custom_call" | custom-call | flops 57500000 | bytes 868352 | tf_op jit(solution)/shard_map/outer/pallas_call | solution.py:640
  15.9 0.1 collective-permute-start.5
  15.9 2.2 %attend.1 = (f32[128,64]{1,0:T(8,128)S(1)}, f32[128,64]{1,0:T(8,128)S(1)}, f32[128,128]{1,0:T(8,128)S(1)}, bf16[128,512]{1,0:T(8,128)(2,1)S(1)}, bf16[128,128]{1...) custom-call(bf16[8,64,128]{2,1,0:T(8,128)(2,1)S(1)} %get-tuple-element.60.refs_0_, ...), custom_call_target="tpu_custom_call" | custom-call | flops 3449999872 | bytes 1351680 | tf_op jit(solution)/shard_map/attend/pallas_call | solution.py:640
  18.1 0.0 collective-permute-done.5.refs_4_
  18.2 2.1 %collective-permute-start.6 = (bf16[384,128]{1,0:T(8,128)(2,1)S(1)}, bf16[384,128]{1,0:T(8,128)(2,1)S(1)}, u32[]{:S(2)}, u32[]{:S(2)}) collective-permute-start(bf16[384,128]{1,0:T(8,128)(2,1)S(1)} %get-tuple-element.77), channel_id=1, source_target_pairs={{0,12},{4,8},{8,4},{12,0},{1,13},{5,9},{9,5},{13,1},{2,14},{6,10},... | collective-permute-start | bytes 294920 | tf_op jit(solution)/shard_map/ppermute | solution.py:595
  20.3 2.4 %collective-permute-start.8 = (bf16[384,128]{1,0:T(8,128)(2,1)S(1)}, bf16[384,128]{1,0:T(8,128)(2,1)S(1)}, u32[]{:S(2)}, u32[]{:S(2)}) collective-permute-start(bf16[384,128]{1,0:T(8,128)(2,1)S(1)} %get-tuple-element.79), channel_id=1, source_target_pairs={{0,4},{4,0},{8,12},{12,8},{1,5},{5,1},{9,13},{13,9},{2,6},{6,2},{1... | collective-permute-start | bytes 294920 | tf_op jit(solution)/shard_map/ppermute | solution.py:595
  22.6 1.3 %collective-permute-done.4.refs_2_ = f32[128,64]{1,0:T(8,128)S(1)} collective-permute-done((f32[128,64]{1,0:T(8,128)S(1)}, f32[128,64]{1,0:T(8,128)S(1)}, u32[]{:S(2)}, u32[]{:S(2)}) %collective-permute-start.4) | collective-permute-done | bytes 32800 | tf_op jit(solution)/shard_map/ppermute | solution.py:591
  23.9 0.2 score.1
  24.1 0.6 %collective-permute-start.11 = (bf16[128,128]{1,0:T(8,128)(2,1)S(1)}, bf16[128,128]{1,0:T(8,128)(2,1)S(1)}, u32[]{:S(2)}, u32[]{:S(2)}) collective-permute-start(bf16[128,128]{1,0:T(8,128)(2,1)S(1)} %get-tuple-element.82), channel_id=1, source_target_pairs={{0,2},{2,0},{1,3},{3,1},{4,6},{6,4},{5,7},{7,5},{8,10},{10,8},{9,1... | collective-permute-start | bytes 98312 | tf_op jit(solution)/shard_map/ppermute | solution.py:591
  24.7 2.8 %own.1.refs_4_.refs_1_ = f32[128,128]{1,0:T(8,128)S(1)} custom-call(bf16[8,64,128]{2,1,0:T(8,128)(2,1)S(1)} %get-tuple-element.60.refs_0_, bf16[16,64,128]{2,1,0:T(8,128)(2,1)S(1)} %get-tuple-element.57.refs_4_.refs_1_, bf16[32,32,128]{2,1,0:T(8,128)(2,1)S(1)} %get-tuple-element.61.refs_2_, bf16[32,64]{1,0:T(8,128)(2,1)S(1)} %get-tuple-element.48.refs_1_.refs_3_, ...), custom_call_target="tpu_custom_call" | custom-call | flops 11500000 | bytes 1069056 | tf_op jit(solution)/shard_map/own/pallas_call | solution.py:640
  27.5 2.2 %collective-permute-done.7.refs_2_.refs_3_ = bf16[384,128]{1,0:T(8,128)(2,1)S(1)} collective-permute-done((bf16[384,128]{1,0:T(8,128)(2,1)S(1)}, bf16[384,128]{1,0:T(8,128)(2,1)S(1)}, u32[]{:S(2)}, u32[]{:S(2)}) %collective-permute-start.7) | collective-permute-done | bytes 98336 | tf_op jit(solution)/shard_map/ppermute | solution.py:595
  29.7 0.1 piece.1.refs_5_.refs_0_
  29.8 0.6 %collective-permute-start.10 = (bf16[256,128]{1,0:T(8,128)(2,1)S(1)}, bf16[256,128]{1,0:T(8,128)(2,1)S(1)}, u32[]{:S(2)}, u32[]{:S(2)}) collective-permute-start(bf16[256,128]{1,0:T(8,128)(2,1)S(1)} %piece.1.refs_5_.refs_0_), channel_id=1, source_target_pairs={{0,2},{2,0},{1,3},{3,1},{4,6},{6,4},{5,7},{7,5},{8,10},{10,8},{9,1... | collective-permute-start | bytes 196616 | tf_op jit(solution)/shard_map/ppermute | solution.py:591
  30.4 0.4 %reduce.1.refs_5_.refs_0_ = bf16[128,128]{1,0:T(8,128)(2,1)S(1)} custom-call(bf16[16,16,64]{2,1,0:T(8,128)(2,1)S(1)} %get-tuple-element.44.refs_0_, f32[128,128]{1,0:T(8,128)S(1)} %own.1.refs_4_.refs_1_, bf16[384,128]{1,0:T(8,128)(2,1)S(1)} %collective-permute-done.6.refs_1_.refs_2_, bf16[384,128]{1,0:T(8,128)(2,1)S(1)} %collective-permute-done.7.refs_2_.refs_3_, ...), custom_call_target="tpu_custom_call" | custom-call | flops 1150000000 | bytes 425984 | tf_op jit(solution)/shard_map/reduce/pallas_call | solution.py:640
  30.8 1.6 %collective-permute-start.9 = (bf16[128,128]{1,0:T(8,128)(2,1)S(1)}, bf16[128,128]{1,0:T(8,128)(2,1)S(1)}, u32[]{:S(2)}, u32[]{:S(2)}) collective-permute-start(bf16[128,128]{1,0:T(8,128)(2,1)S(1)} %reduce.1.refs_5_.refs_0_), channel_id=1, source_target_pairs={{0,2},{2,0},{1,3},{3,1},{4,6},{6,4},{5,7},{7,5},{8,10},{10,8},{9,1... | collective-permute-start | bytes 98312 | tf_op jit(solution)/shard_map/ppermute | solution.py:591
  32.3 1.7 %pair.1.refs_2_ = bf16[16,32,128]{2,1,0:T(8,128)(2,1)} custom-call(bf16[16,32,128]{2,1,0:T(8,128)(2,1)S(1)} %get-tuple-element.80.refs_0_, bf16[8,128]{1,0:T(8,128)(2,1)S(1)} %get-tuple-element.81.refs_1_, f32[128,64]{1,0:T(8,128)S(1)} %get-tuple-element.68.refs_0_.refs_2_, f32[128,33]{1,0:T(8,128)S(1)} %get-tuple-element.76.refs_9_.refs_3_, ...), custom_call_target="tpu_custom_call" | custom-call | flops 11500000 | bytes 346624 | tf_op jit(solution)/shard_map/pair/pallas_call | solution.py:640
  34.0 0.2 collective-permute-done.10.refs_1_
  34.2 0.1 collective-permute-start.12
  34.3 0.4 %collective-permute-done.9.refs_1_ = bf16[128,128]{1,0:T(8,128)(2,1)S(1)} collective-permute-done((bf16[128,128]{1,0:T(8,128)(2,1)S(1)}, bf16[128,128]{1,0:T(8,128)(2,1)S(1)}, u32[]{:S(2)}, u32[]{:S(2)}) %collective-permute-start.9) | collective-permute-done | bytes 32800 | tf_op jit(solution)/shard_map/ppermute | solution.py:591
  34.7 0.1 unpack.1.refs_0_
  34.8 0.8 %collective-permute-done.12.refs_2_ = bf16[2,16,16,128]{3,2,1,0:T(8,128)(2,1)S(1)} collective-permute-done((bf16[2,16,16,128]{3,2,1,0:T(8,128)(2,1)S(1)}, bf16[2,16,16,128]{3,2,1,0:T(8,128)(2,1)S(1)}, u32[]{:S(2)}, u32[]{:S(2)}) %collective-permute-start.12) | collective-permute-done | bytes 131104 | tf_op jit(solution)/shard_map/ppermute | solution.py:591
  35.7 0.9 %finish.1 = (bf16[32,16,64]{2,1,0:T(8,128)(2,1)}, f32[32,32,128]{2,1,0:T(8,128)}) custom-call(bf16[32,16,64]{2,1,0:T(8,128)(2,1)S(1)} %unpack.1.refs_0_, bf16[2,16,16,128]{3,2,1,0:T(8,128)(2,1)S(1)} %bitcast.11, bf16[2,16,16,128]{3,2,1,0:T(8,128)(2,1)S(1)} %collective-permute-done.12.refs_2_), custom_call_target="tpu_custom_call" | custom-call | flops 1150000000 | bytes 917504 | tf_op jit(solution)/shard_map/finish/pallas_call | solution.py:640
  (9 shorter events, 0.1 us)
Async XLA Ops:
  2.8 8.7 %collective-permute-start.3 = (bf16[608,128]{1,0:T(8,128)(2,1)S(1)}, bf16[608,128]{1,0:T(8,128)(2,1)S(1)}, u32[]{:S(2)}, u32[]{:S(2)}) collective-permute-start(bf16[608,128]{1,0:T(8,128)(2,1)S(1)} %get-tuple-element.46.refs_0_), channel_id=1, source_target_pairs={{0,2},{2,0},{1,3},{3,1},{4,6},{6,4},{5,7},{7,5},{8,10},{10,8},{9,1... | collective-permute-start | bytes 466952 | tf_op jit(solution)/shard_map/ppermute | solution.py:591
  5.8 7.1 %collective-permute-start = (bf16[160,128]{1,0:T(8,128)(2,1)S(1)}, bf16[160,128]{1,0:T(8,128)(2,1)S(1)}, u32[]{:S(2)}, u32[]{:S(2)}) collective-permute-start(bf16[160,128]{1,0:T(8,128)(2,1)S(1)} %get-tuple-element.45.refs_0_), channel_id=1, source_target_pairs={{0,8},{4,12},{8,0},{12,4},{1,9},{5,13},{9,1},{13,5},{2,10},{6,14},... | collective-permute-start | bytes 122888 | tf_op jit(solution)/shard_map/ppermute | solution.py:595
  8.4 5.8 %collective-permute-start.1 = (bf16[160,128]{1,0:T(8,128)(2,1)S(1)}, bf16[160,128]{1,0:T(8,128)(2,1)S(1)}, u32[]{:S(2)}, u32[]{:S(2)}) collective-permute-start(bf16[160,128]{1,0:T(8,128)(2,1)S(1)} %get-tuple-element.45.refs_0_), channel_id=1, source_target_pairs={{0,12},{4,8},{8,4},{12,0},{1,13},{5,9},{9,5},{13,1},{2,14},{6,10},... | collective-permute-start | bytes 122888 | tf_op jit(solution)/shard_map/ppermute | solution.py:595
  9.8 4.5 %collective-permute-start.2 = (bf16[160,128]{1,0:T(8,128)(2,1)S(1)}, bf16[160,128]{1,0:T(8,128)(2,1)S(1)}, u32[]{:S(2)}, u32[]{:S(2)}) collective-permute-start(bf16[160,128]{1,0:T(8,128)(2,1)S(1)} %get-tuple-element.45.refs_0_), channel_id=1, source_target_pairs={{0,4},{4,0},{8,12},{12,8},{1,5},{5,1},{9,13},{13,9},{2,6},{6,2},{1... | collective-permute-start | bytes 122888 | tf_op jit(solution)/shard_map/ppermute | solution.py:595
  15.9 2.3 %collective-permute-start.5 = (f32[256,128]{1,0:T(8,128)S(1)}, f32[256,128]{1,0:T(8,128)S(1)}, u32[]{:S(2)}, u32[]{:S(2)}) collective-permute-start(f32[256,128]{1,0:T(8,128)S(1)} %get-tuple-element.74), channel_id=1, source_target_pairs={{0,1},{1,0},{2,3},{3,2},{4,5},{5,4},{6,7},{7,6},{8,9},{9,8},{10,11... | collective-permute-start | bytes 393224 | tf_op jit(solution)/shard_map/ppermute | solution.py:591
  18.2 9.3 %collective-permute-start.6 = (bf16[384,128]{1,0:T(8,128)(2,1)S(1)}, bf16[384,128]{1,0:T(8,128)(2,1)S(1)}, u32[]{:S(2)}, u32[]{:S(2)}) collective-permute-start(bf16[384,128]{1,0:T(8,128)(2,1)S(1)} %get-tuple-element.77), channel_id=1, source_target_pairs={{0,12},{4,8},{8,4},{12,0},{1,13},{5,9},{9,5},{13,1},{2,14},{6,10},... | collective-permute-start | bytes 294920 | tf_op jit(solution)/shard_map/ppermute | solution.py:595
  20.3 9.4 %collective-permute-start.7 = (bf16[384,128]{1,0:T(8,128)(2,1)S(1)}, bf16[384,128]{1,0:T(8,128)(2,1)S(1)}, u32[]{:S(2)}, u32[]{:S(2)}) collective-permute-start(bf16[384,128]{1,0:T(8,128)(2,1)S(1)} %get-tuple-element.78), channel_id=1, source_target_pairs={{0,8},{4,12},{8,0},{12,4},{1,9},{5,13},{9,1},{13,5},{2,10},{6,14},... | collective-permute-start | bytes 294920 | tf_op jit(solution)/shard_map/ppermute | solution.py:595
  20.3 9.4 %collective-permute-start.8 = (bf16[384,128]{1,0:T(8,128)(2,1)S(1)}, bf16[384,128]{1,0:T(8,128)(2,1)S(1)}, u32[]{:S(2)}, u32[]{:S(2)}) collective-permute-start(bf16[384,128]{1,0:T(8,128)(2,1)S(1)} %get-tuple-element.79), channel_id=1, source_target_pairs={{0,4},{4,0},{8,12},{12,8},{1,5},{5,1},{9,13},{13,9},{2,6},{6,2},{1... | collective-permute-start | bytes 294920 | tf_op jit(solution)/shard_map/ppermute | solution.py:595
  22.6 1.3 %collective-permute-start.4 = (f32[128,64]{1,0:T(8,128)S(1)}, f32[128,64]{1,0:T(8,128)S(1)}, u32[]{:S(2)}, u32[]{:S(2)}) collective-permute-start(f32[128,64]{1,0:T(8,128)S(1)} %get-tuple-element.69.refs_1_), channel_id=1, source_target_pairs={{0,1},{1,0},{2,3},{3,2},{4,5},{5,4},{6,7},{7,6},{8,9},{9,8},{10,11... | collective-permute-start | bytes 98312 | tf_op jit(solution)/shard_map/ppermute | solution.py:591
  24.1 8.2 %collective-permute-start.11 = (bf16[128,128]{1,0:T(8,128)(2,1)S(1)}, bf16[128,128]{1,0:T(8,128)(2,1)S(1)}, u32[]{:S(2)}, u32[]{:S(2)}) collective-permute-start(bf16[128,128]{1,0:T(8,128)(2,1)S(1)} %get-tuple-element.82), channel_id=1, source_target_pairs={{0,2},{2,0},{1,3},{3,1},{4,6},{6,4},{5,7},{7,5},{8,10},{10,8},{9,1... | collective-permute-start | bytes 98312 | tf_op jit(solution)/shard_map/ppermute | solution.py:591
  29.8 4.4 %collective-permute-start.10 = (bf16[256,128]{1,0:T(8,128)(2,1)S(1)}, bf16[256,128]{1,0:T(8,128)(2,1)S(1)}, u32[]{:S(2)}, u32[]{:S(2)}) collective-permute-start(bf16[256,128]{1,0:T(8,128)(2,1)S(1)} %piece.1.refs_5_.refs_0_), channel_id=1, source_target_pairs={{0,2},{2,0},{1,3},{3,1},{4,6},{6,4},{5,7},{7,5},{8,10},{10,8},{9,1... | collective-permute-start | bytes 196616 | tf_op jit(solution)/shard_map/ppermute | solution.py:591
  30.8 4.0 %collective-permute-start.9 = (bf16[128,128]{1,0:T(8,128)(2,1)S(1)}, bf16[128,128]{1,0:T(8,128)(2,1)S(1)}, u32[]{:S(2)}, u32[]{:S(2)}) collective-permute-start(bf16[128,128]{1,0:T(8,128)(2,1)S(1)} %reduce.1.refs_5_.refs_0_), channel_id=1, source_target_pairs={{0,2},{2,0},{1,3},{3,1},{4,6},{6,4},{5,7},{7,5},{8,10},{10,8},{9,1... | collective-permute-start | bytes 98312 | tf_op jit(solution)/shard_map/ppermute | solution.py:591
  34.2 1.4 %collective-permute-start.12 = (bf16[2,16,16,128]{3,2,1,0:T(8,128)(2,1)S(1)}, bf16[2,16,16,128]{3,2,1,0:T(8,128)(2,1)S(1)}, u32[]{:S(2)}, u32[]{:S(2)}) collective-permute-start(bf16[2,16,16,128]{3,2,1,0:T(8,128)(2,1)S(1)} %bitcast.9), channel_id=1, source_target_pairs={{0,1},{1,0},{2,3},{3,2},{4,5},{5,4},{6,7},{7,6},{8,9},{9,8},{10,11... | collective-permute-start | bytes 393224 | tf_op jit(solution)/shard_map/ppermute | solution.py:591

commit v2 on v1

--- a/solution.py
+++ b/solution.py
@@ -114,7 +114,8 @@
     ]
     for copy in copies:
         copy.start()
-    copies[5].wait()
+    for copy in (*copies[:4], copies[5], *copies[8:]):
+        copy.wait()
     lane = iota((1, 2 * g.M), 1)
     groups = [lax.rem(col + m, g.C) for m in range(g.C)]
     for m, group in enumerate(groups):
@@ -126,11 +127,8 @@
             else:
                 flags = jnp.zeros((1, 2 * g.M), F32)
             mask_ref[m * g.SP + k : m * g.SP + k + 1, :] = flags
-    copies[9].wait()
     count = jnp.sum(every_in[...].astype(F32), -1, keepdims=True)
     mask_ref[g.C * g.SP : g.C * g.SP + 1, :] = jnp.broadcast_to(1.0 / (0.001 + count), (1, 2 * g.M))
-    copies[0].wait()
-    copies[8].wait()
     norm_ref[...] = standardize(x_in[...].astype(F32))[0]
     x_ref[...] = x_in[pl.ds(col * g.SQ, g.SQ)]
     second = column_weights(g, w2_ref[...])
@@ -154,8 +152,6 @@
         for k in range(g.EXTRA):
             block = wide[:, k * LANES : (k + 1) * LANES]
             send_ref[rows + k * g.I : rows + (k + 1) * g.I, :] = block.astype(BF16)
-    for copy in copies[1:4]:
-        copy.wait()
     pair = standardize(e_ref[...].astype(F32).reshape(pairs, g.Z))[0].astype(BF16)
     penalty = (flag_in[...].astype(F32) - 1.0) * PENALTY
     weights = wl_ref[...]

time: 36.7 us -> 36.4 us (level)
  no operation moved by 1% of the time
where the time goes in v2:
time: 36.4 us; the launch traced here: 36.2 us
  Pallas kernels  14.7 us (40%)
  starting transfers between devices  14.5 us (40%)
  waiting for transfers between devices  6.19 us (17%)
  between operations  0.78 us (2%)
    pallas_call x15, Pallas kernels, call(): pl.pallas_call(body, out_shape=outs[0] if single else tuple(outs), in_spe...  14.7 us
    ppermute x6, starting transfers between devices, swap(): lax.ppermute(array, axis, [(i, i ^ x) for i in range(lax.axis_size(axis))])  8.62 us
    ppermute x7, starting transfers between devices, shift(): lax.ppermute(array, axis, [(i, (i + k) % count) for i in range(count)])  5.92 us
    ppermute x6, waiting for transfers between devices, swap(): lax.ppermute(array, axis, [(i, i ^ x) for i in range(lax.axis_size(axis))])  3.48 us
    ppermute x7, waiting for transfers between devices, shift(): lax.ppermute(array, axis, [(i, (i + k) % count) for i in range(count)])  2.71 us
  transfers between devices with their start and end apart: 13, of which 6 were waited for; matrix products, arithmetic and copies ran while one was open for 0% of the time, Pallas kernels for 28%

profile of v2, /device:TPU:0, one launch (start us, length us, event | category | flops | bytes accessed | tf_op | source)
XLA Modules:
  0.0 36.2 jit_solution(12420477158839024159)
XLA Ops:
  0.6 1.9 %normalise.1 = (bf16[2,8,16,128]{3,2,1,0:T(8,128)(2,1)S(1)}, bf16[160,128]{1,0:T(8,128)(2,1)S(1)}, f32[32,128]{1,0:T(8,128)S(1)}, bf16[608,128]{1,0:T(8,128)(2,1...) custom-call(bf16[32,16,64]{2,1,0:T(8,128)(2,1)} %refs_0_.1, ...), custom_call_target="tpu_custom_call" | custom-call | flops 2300000000 | bytes 1327744 | tf_op jit(solution)/shard_map/normalise/pallas_call | solution.py:636
  2.5 3.0 %collective-permute-start.3 = (bf16[608,128]{1,0:T(8,128)(2,1)S(1)}, bf16[608,128]{1,0:T(8,128)(2,1)S(1)}, u32[]{:S(2)}, u32[]{:S(2)}) collective-permute-start(bf16[608,128]{1,0:T(8,128)(2,1)S(1)} %get-tuple-element.46.refs_0_), channel_id=1, source_target_pairs={{0,2},{2,0},{1,3},{3,1},{4,6},{6,4},{5,7},{7,5},{8,10},{10,8},{9,1... | collective-permute-start | bytes 466952 | tf_op jit(solution)/shard_map/ppermute | solution.py:587
  5.5 2.6 %collective-permute-start = (bf16[160,128]{1,0:T(8,128)(2,1)S(1)}, bf16[160,128]{1,0:T(8,128)(2,1)S(1)}, u32[]{:S(2)}, u32[]{:S(2)}) collective-permute-start(bf16[160,128]{1,0:T(8,128)(2,1)S(1)} %get-tuple-element.45.refs_0_), channel_id=1, source_target_pairs={{0,8},{4,12},{8,0},{12,4},{1,9},{5,13},{9,1},{13,5},{2,10},{6,14},... | collective-permute-start | bytes 122888 | tf_op jit(solution)/shard_map/ppermute | solution.py:591
  8.1 1.3 %collective-permute-start.1 = (bf16[160,128]{1,0:T(8,128)(2,1)S(1)}, bf16[160,128]{1,0:T(8,128)(2,1)S(1)}, u32[]{:S(2)}, u32[]{:S(2)}) collective-permute-start(bf16[160,128]{1,0:T(8,128)(2,1)S(1)} %get-tuple-element.45.refs_0_), channel_id=1, source_target_pairs={{0,12},{4,8},{8,4},{12,0},{1,13},{5,9},{9,5},{13,1},{2,14},{6,10},... | collective-permute-start | bytes 122888 | tf_op jit(solution)/shard_map/ppermute | solution.py:591
  9.4 0.2 collective-permute-start.2
  9.7 1.5 %prepare.1 = (bf16[512,32]{1,0:T(8,128)(2,1)S(1)}, bf16[32,32,128]{2,1,0:T(8,128)(2,1)S(1)}, bf16[16,512,128]{2,1,0:T(8,128)(2,1)S(1)}, bf16[16,16,64]{2,1,0:T(8...) custom-call(bf16[2,8,16,128]{3,2,1,0:T(8,128)(2,1)S(1)} %get-tuple-element.47., ...), custom_call_target="tpu_custom_call" | custom-call | flops 11500000 | bytes 3031040 | tf_op jit(solution)/shard_map/prepare/pallas_call | solution.py:636
  11.2 0.0 collective-permute-done.3.refs_4_.refs_1_.refs_2_
  11.2 0.2 gate.1
  11.5 1.1 %right.1 = (bf16[16,64,128]{2,1,0:T(8,128)(2,1)S(1)}, f32[8,64,128]{2,1,0:T(8,128)S(1)}) custom-call(bf16[608,128]{1,0:T(8,128)(2,1)S(1)} %get-tuple-element.46.refs_0_, bf16[608,128]{1,0:T(8,128)(2,1)S(1)} %collective-permute-done.3.refs_4_.refs_1_.refs_2_, bf16[16,512,128]{2,1,0:T(8,128)(2,1)S(1)} %get-tuple-element.51.refs_2_, ...), custom_call_target="tpu_custom_call" | custom-call | flops 11500000 | bytes 2949120 | tf_op jit(solution)/shard_map/right/pallas_call | solution.py:636
  12.6 0.0 collective-permute-done.refs_1_
  12.6 1.3 %collective-permute-done.1.refs_2_ = bf16[160,128]{1,0:T(8,128)(2,1)S(1)} collective-permute-done((bf16[160,128]{1,0:T(8,128)(2,1)S(1)}, bf16[160,128]{1,0:T(8,128)(2,1)S(1)}, u32[]{:S(2)}, u32[]{:S(2)}) %collective-permute-start.1) | collective-permute-done | bytes 40992 | tf_op jit(solution)/shard_map/ppermute | solution.py:591
  13.9 1.6 %outer.1 = (bf16[8,64,128]{2,1,0:T(8,128)(2,1)S(1)}, f32[256,128]{1,0:T(8,128)S(1)}, f32[256,128]{1,0:T(8,128)S(1)}) custom-call(bf16[160,128]{1,0:T(8,128)(2,1)S(1)} %get-tuple-element.45.refs_0_, bf16[160,128]{1,0:T(8,128)(2,1)S(1)} %collective-permute-done.refs_1_, bf16[160,128]{1,0:T(8,128)(2,1)S(1)} %collective-permute-done.1.refs_2_, ...), custom_call_target="tpu_custom_call" | custom-call | flops 57500000 | bytes 868352 | tf_op jit(solution)/shard_map/outer/pallas_call | solution.py:636
  15.5 0.1 collective-permute-start.5
  15.6 2.2 %attend.1 = (f32[128,64]{1,0:T(8,128)S(1)}, f32[128,64]{1,0:T(8,128)S(1)}, f32[128,128]{1,0:T(8,128)S(1)}, bf16[128,512]{1,0:T(8,128)(2,1)S(1)}, bf16[128,128]{1...) custom-call(bf16[8,64,128]{2,1,0:T(8,128)(2,1)S(1)} %get-tuple-element.60.refs_0_, ...), custom_call_target="tpu_custom_call" | custom-call | flops 3449999872 | bytes 1351680 | tf_op jit(solution)/shard_map/attend/pallas_call | solution.py:636
  17.9 2.1 %collective-permute-start.6 = (bf16[384,128]{1,0:T(8,128)(2,1)S(1)}, bf16[384,128]{1,0:T(8,128)(2,1)S(1)}, u32[]{:S(2)}, u32[]{:S(2)}) collective-permute-start(bf16[384,128]{1,0:T(8,128)(2,1)S(1)} %get-tuple-element.77), channel_id=1, source_target_pairs={{0,12},{4,8},{8,4},{12,0},{1,13},{5,9},{9,5},{13,1},{2,14},{6,10},... | collective-permute-start | bytes 294920 | tf_op jit(solution)/shard_map/ppermute | solution.py:591
  20.0 2.4 %collective-permute-start.8 = (bf16[384,128]{1,0:T(8,128)(2,1)S(1)}, bf16[384,128]{1,0:T(8,128)(2,1)S(1)}, u32[]{:S(2)}, u32[]{:S(2)}) collective-permute-start(bf16[384,128]{1,0:T(8,128)(2,1)S(1)} %get-tuple-element.79), channel_id=1, source_target_pairs={{0,4},{4,0},{8,12},{12,8},{1,5},{5,1},{9,13},{13,9},{2,6},{6,2},{1... | collective-permute-start | bytes 294920 | tf_op jit(solution)/shard_map/ppermute | solution.py:591
  22.3 1.3 %collective-permute-done.4.refs_2_ = f32[128,64]{1,0:T(8,128)S(1)} collective-permute-done((f32[128,64]{1,0:T(8,128)S(1)}, f32[128,64]{1,0:T(8,128)S(1)}, u32[]{:S(2)}, u32[]{:S(2)}) %collective-permute-start.4) | collective-permute-done | bytes 32800 | tf_op jit(solution)/shard_map/ppermute | solution.py:587
  23.6 0.2 score.1
  23.8 0.6 %collective-permute-start.11 = (bf16[128,128]{1,0:T(8,128)(2,1)S(1)}, bf16[128,128]{1,0:T(8,128)(2,1)S(1)}, u32[]{:S(2)}, u32[]{:S(2)}) collective-permute-start(bf16[128,128]{1,0:T(8,128)(2,1)S(1)} %get-tuple-element.82), channel_id=1, source_target_pairs={{0,2},{2,0},{1,3},{3,1},{4,6},{6,4},{5,7},{7,5},{8,10},{10,8},{9,1... | collective-permute-start | bytes 98312 | tf_op jit(solution)/shard_map/ppermute | solution.py:587
  24.4 2.8 %own.1.refs_4_.refs_1_ = f32[128,128]{1,0:T(8,128)S(1)} custom-call(bf16[8,64,128]{2,1,0:T(8,128)(2,1)S(1)} %get-tuple-element.60.refs_0_, bf16[16,64,128]{2,1,0:T(8,128)(2,1)S(1)} %get-tuple-element.57.refs_4_.refs_1_, bf16[32,32,128]{2,1,0:T(8,128)(2,1)S(1)} %get-tuple-element.61.refs_2_, bf16[32,64]{1,0:T(8,128)(2,1)S(1)} %get-tuple-element.48.refs_1_.refs_3_, ...), custom_call_target="tpu_custom_call" | custom-call | flops 11500000 | bytes 1069056 | tf_op jit(solution)/shard_map/own/pallas_call | solution.py:636
  27.2 2.2 %collective-permute-done.7.refs_2_.refs_3_ = bf16[384,128]{1,0:T(8,128)(2,1)S(1)} collective-permute-done((bf16[384,128]{1,0:T(8,128)(2,1)S(1)}, bf16[384,128]{1,0:T(8,128)(2,1)S(1)}, u32[]{:S(2)}, u32[]{:S(2)}) %collective-permute-start.7) | collective-permute-done | bytes 98336 | tf_op jit(solution)/shard_map/ppermute | solution.py:591
  29.4 0.1 piece.1.refs_5_.refs_0_
  29.5 0.6 %collective-permute-start.10 = (bf16[256,128]{1,0:T(8,128)(2,1)S(1)}, bf16[256,128]{1,0:T(8,128)(2,1)S(1)}, u32[]{:S(2)}, u32[]{:S(2)}) collective-permute-start(bf16[256,128]{1,0:T(8,128)(2,1)S(1)} %piece.1.refs_5_.refs_0_), channel_id=1, source_target_pairs={{0,2},{2,0},{1,3},{3,1},{4,6},{6,4},{5,7},{7,5},{8,10},{10,8},{9,1... | collective-permute-start | bytes 196616 | tf_op jit(solution)/shard_map/ppermute | solution.py:587
  30.0 0.4 %reduce.1.refs_5_.refs_0_ = bf16[128,128]{1,0:T(8,128)(2,1)S(1)} custom-call(bf16[16,16,64]{2,1,0:T(8,128)(2,1)S(1)} %get-tuple-element.44.refs_0_, f32[128,128]{1,0:T(8,128)S(1)} %own.1.refs_4_.refs_1_, bf16[384,128]{1,0:T(8,128)(2,1)S(1)} %collective-permute-done.6.refs_1_.refs_2_, bf16[384,128]{1,0:T(8,128)(2,1)S(1)} %collective-permute-done.7.refs_2_.refs_3_, ...), custom_call_target="tpu_custom_call" | custom-call | flops 1150000000 | bytes 425984 | tf_op jit(solution)/shard_map/reduce/pallas_call | solution.py:636
  30.4 1.6 %collective-permute-start.9 = (bf16[128,128]{1,0:T(8,128)(2,1)S(1)}, bf16[128,128]{1,0:T(8,128)(2,1)S(1)}, u32[]{:S(2)}, u32[]{:S(2)}) collective-permute-start(bf16[128,128]{1,0:T(8,128)(2,1)S(1)} %reduce.1.refs_5_.refs_0_), channel_id=1, source_target_pairs={{0,2},{2,0},{1,3},{3,1},{4,6},{6,4},{5,7},{7,5},{8,10},{10,8},{9,1... | collective-permute-start | bytes 98312 | tf_op jit(solution)/shard_map/ppermute | solution.py:587
  32.0 1.7 %pair.1.refs_2_ = bf16[16,32,128]{2,1,0:T(8,128)(2,1)} custom-call(bf16[16,32,128]{2,1,0:T(8,128)(2,1)S(1)} %get-tuple-element.80.refs_0_, bf16[8,128]{1,0:T(8,128)(2,1)S(1)} %get-tuple-element.81.refs_1_, f32[128,64]{1,0:T(8,128)S(1)} %get-tuple-element.68.refs_0_.refs_2_, f32[128,33]{1,0:T(8,128)S(1)} %get-tuple-element.76.refs_9_.refs_3_, ...), custom_call_target="tpu_custom_call" | custom-call | flops 11500000 | bytes 346624 | tf_op jit(solution)/shard_map/pair/pallas_call | solution.py:636
  33.7 0.2 collective-permute-done.10.refs_1_
  33.9 0.1 collective-permute-start.12
  34.0 0.4 %collective-permute-done.9.refs_1_ = bf16[128,128]{1,0:T(8,128)(2,1)S(1)} collective-permute-done((bf16[128,128]{1,0:T(8,128)(2,1)S(1)}, bf16[128,128]{1,0:T(8,128)(2,1)S(1)}, u32[]{:S(2)}, u32[]{:S(2)}) %collective-permute-start.9) | collective-permute-done | bytes 32800 | tf_op jit(solution)/shard_map/ppermute | solution.py:587
  34.4 0.1 unpack.1.refs_0_
  34.5 0.9 %collective-permute-done.12.refs_2_ = bf16[2,16,16,128]{3,2,1,0:T(8,128)(2,1)S(1)} collective-permute-done((bf16[2,16,16,128]{3,2,1,0:T(8,128)(2,1)S(1)}, bf16[2,16,16,128]{3,2,1,0:T(8,128)(2,1)S(1)}, u32[]{:S(2)}, u32[]{:S(2)}) %collective-permute-start.12) | collective-permute-done | bytes 131104 | tf_op jit(solution)/shard_map/ppermute | solution.py:587
  35.3 0.9 %finish.1 = (bf16[32,16,64]{2,1,0:T(8,128)(2,1)}, f32[32,32,128]{2,1,0:T(8,128)}) custom-call(bf16[32,16,64]{2,1,0:T(8,128)(2,1)S(1)} %unpack.1.refs_0_, bf16[2,16,16,128]{3,2,1,0:T(8,128)(2,1)S(1)} %bitcast.11, bf16[2,16,16,128]{3,2,1,0:T(8,128)(2,1)S(1)} %collective-permute-done.12.refs_2_), custom_call_target="tpu_custom_call" | custom-call | flops 1150000000 | bytes 917504 | tf_op jit(solution)/shard_map/finish/pallas_call | solution.py:636
  (9 shorter events, 0.1 us)
Async XLA Ops:
  2.5 8.7 %collective-permute-start.3 = (bf16[608,128]{1,0:T(8,128)(2,1)S(1)}, bf16[608,128]{1,0:T(8,128)(2,1)S(1)}, u32[]{:S(2)}, u32[]{:S(2)}) collective-permute-start(bf16[608,128]{1,0:T(8,128)(2,1)S(1)} %get-tuple-element.46.refs_0_), channel_id=1, source_target_pairs={{0,2},{2,0},{1,3},{3,1},{4,6},{6,4},{5,7},{7,5},{8,10},{10,8},{9,1... | collective-permute-start | bytes 466952 | tf_op jit(solution)/shard_map/ppermute | solution.py:587
  5.5 7.1 %collective-permute-start = (bf16[160,128]{1,0:T(8,128)(2,1)S(1)}, bf16[160,128]{1,0:T(8,128)(2,1)S(1)}, u32[]{:S(2)}, u32[]{:S(2)}) collective-permute-start(bf16[160,128]{1,0:T(8,128)(2,1)S(1)} %get-tuple-element.45.refs_0_), channel_id=1, source_target_pairs={{0,8},{4,12},{8,0},{12,4},{1,9},{5,13},{9,1},{13,5},{2,10},{6,14},... | collective-permute-start | bytes 122888 | tf_op jit(solution)/shard_map/ppermute | solution.py:591
  8.1 5.8 %collective-permute-start.1 = (bf16[160,128]{1,0:T(8,128)(2,1)S(1)}, bf16[160,128]{1,0:T(8,128)(2,1)S(1)}, u32[]{:S(2)}, u32[]{:S(2)}) collective-permute-start(bf16[160,128]{1,0:T(8,128)(2,1)S(1)} %get-tuple-element.45.refs_0_), channel_id=1, source_target_pairs={{0,12},{4,8},{8,4},{12,0},{1,13},{5,9},{9,5},{13,1},{2,14},{6,10},... | collective-permute-start | bytes 122888 | tf_op jit(solution)/shard_map/ppermute | solution.py:591
  9.4 4.5 %collective-permute-start.2 = (bf16[160,128]{1,0:T(8,128)(2,1)S(1)}, bf16[160,128]{1,0:T(8,128)(2,1)S(1)}, u32[]{:S(2)}, u32[]{:S(2)}) collective-permute-start(bf16[160,128]{1,0:T(8,128)(2,1)S(1)} %get-tuple-element.45.refs_0_), channel_id=1, source_target_pairs={{0,4},{4,0},{8,12},{12,8},{1,5},{5,1},{9,13},{13,9},{2,6},{6,2},{1... | collective-permute-start | bytes 122888 | tf_op jit(solution)/shard_map/ppermute | solution.py:591
  15.5 2.3 %collective-permute-start.5 = (f32[256,128]{1,0:T(8,128)S(1)}, f32[256,128]{1,0:T(8,128)S(1)}, u32[]{:S(2)}, u32[]{:S(2)}) collective-permute-start(f32[256,128]{1,0:T(8,128)S(1)} %get-tuple-element.74), channel_id=1, source_target_pairs={{0,1},{1,0},{2,3},{3,2},{4,5},{5,4},{6,7},{7,6},{8,9},{9,8},{10,11... | collective-permute-start | bytes 393224 | tf_op jit(solution)/shard_map/ppermute | solution.py:587
  17.9 9.3 %collective-permute-start.6 = (bf16[384,128]{1,0:T(8,128)(2,1)S(1)}, bf16[384,128]{1,0:T(8,128)(2,1)S(1)}, u32[]{:S(2)}, u32[]{:S(2)}) collective-permute-start(bf16[384,128]{1,0:T(8,128)(2,1)S(1)} %get-tuple-element.77), channel_id=1, source_target_pairs={{0,12},{4,8},{8,4},{12,0},{1,13},{5,9},{9,5},{13,1},{2,14},{6,10},... | collective-permute-start | bytes 294920 | tf_op jit(solution)/shard_map/ppermute | solution.py:591
  20.0 9.4 %collective-permute-start.7 = (bf16[384,128]{1,0:T(8,128)(2,1)S(1)}, bf16[384,128]{1,0:T(8,128)(2,1)S(1)}, u32[]{:S(2)}, u32[]{:S(2)}) collective-permute-start(bf16[384,128]{1,0:T(8,128)(2,1)S(1)} %get-tuple-element.78), channel_id=1, source_target_pairs={{0,8},{4,12},{8,0},{12,4},{1,9},{5,13},{9,1},{13,5},{2,10},{6,14},... | collective-permute-start | bytes 294920 | tf_op jit(solution)/shard_map/ppermute | solution.py:591
  20.0 9.4 %collective-permute-start.8 = (bf16[384,128]{1,0:T(8,128)(2,1)S(1)}, bf16[384,128]{1,0:T(8,128)(2,1)S(1)}, u32[]{:S(2)}, u32[]{:S(2)}) collective-permute-start(bf16[384,128]{1,0:T(8,128)(2,1)S(1)} %get-tuple-element.79), channel_id=1, source_target_pairs={{0,4},{4,0},{8,12},{12,8},{1,5},{5,1},{9,13},{13,9},{2,6},{6,2},{1... | collective-permute-start | bytes 294920 | tf_op jit(solution)/shard_map/ppermute | solution.py:591
  22.3 1.3 %collective-permute-start.4 = (f32[128,64]{1,0:T(8,128)S(1)}, f32[128,64]{1,0:T(8,128)S(1)}, u32[]{:S(2)}, u32[]{:S(2)}) collective-permute-start(f32[128,64]{1,0:T(8,128)S(1)} %get-tuple-element.69.refs_1_), channel_id=1, source_target_pairs={{0,1},{1,0},{2,3},{3,2},{4,5},{5,4},{6,7},{7,6},{8,9},{9,8},{10,11... | collective-permute-start | bytes 98312 | tf_op jit(solution)/shard_map/ppermute | solution.py:587
  23.8 8.2 %collective-permute-start.11 = (bf16[128,128]{1,0:T(8,128)(2,1)S(1)}, bf16[128,128]{1,0:T(8,128)(2,1)S(1)}, u32[]{:S(2)}, u32[]{:S(2)}) collective-permute-start(bf16[128,128]{1,0:T(8,128)(2,1)S(1)} %get-tuple-element.82), channel_id=1, source_target_pairs={{0,2},{2,0},{1,3},{3,1},{4,6},{6,4},{5,7},{7,5},{8,10},{10,8},{9,1... | collective-permute-start | bytes 98312 | tf_op jit(solution)/shard_map/ppermute | solution.py:587
  29.5 4.5 %collective-permute-start.10 = (bf16[256,128]{1,0:T(8,128)(2,1)S(1)}, bf16[256,128]{1,0:T(8,128)(2,1)S(1)}, u32[]{:S(2)}, u32[]{:S(2)}) collective-permute-start(bf16[256,128]{1,0:T(8,128)(2,1)S(1)} %piece.1.refs_5_.refs_0_), channel_id=1, source_target_pairs={{0,2},{2,0},{1,3},{3,1},{4,6},{6,4},{5,7},{7,5},{8,10},{10,8},{9,1... | collective-permute-start | bytes 196616 | tf_op jit(solution)/shard_map/ppermute | solution.py:587
  30.4 4.0 %collective-permute-start.9 = (bf16[128,128]{1,0:T(8,128)(2,1)S(1)}, bf16[128,128]{1,0:T(8,128)(2,1)S(1)}, u32[]{:S(2)}, u32[]{:S(2)}) collective-permute-start(bf16[128,128]{1,0:T(8,128)(2,1)S(1)} %reduce.1.refs_5_.refs_0_), channel_id=1, source_target_pairs={{0,2},{2,0},{1,3},{3,1},{4,6},{6,4},{5,7},{7,5},{8,10},{10,8},{9,1... | collective-permute-start | bytes 98312 | tf_op jit(solution)/shard_map/ppermute | solution.py:587
  33.9 1.4 %collective-permute-start.12 = (bf16[2,16,16,128]{3,2,1,0:T(8,128)(2,1)S(1)}, bf16[2,16,16,128]{3,2,1,0:T(8,128)(2,1)S(1)}, u32[]{:S(2)}, u32[]{:S(2)}) collective-permute-start(bf16[2,16,16,128]{3,2,1,0:T(8,128)(2,1)S(1)} %bitcast.9), channel_id=1, source_target_pairs={{0,1},{1,0},{2,3},{3,2},{4,5},{5,4},{6,7},{7,6},{8,9},{9,8},{10,11... | collective-permute-start | bytes 393224 | tf_op jit(solution)/shard_map/ppermute | solution.py:587

commit v3 on v2

--- a/solution.py
+++ b/solution.py
@@ -268,8 +268,8 @@
 def outer_kernel(g, *refs):
     refs = list(refs)
     x_refs, refs = refs[: g.R], refs[g.R :]
-    d_ref, left_ref, w2_ref, mask_ref, xall_ref, *refs = refs
-    w_refs, (others_ref, spread_ref, rt_ref, ds_ref, all_ref) = refs[: g.D], refs[g.D :]
+    d_ref, left_ref, w2_ref, mask_ref, xall_ref, ds_ref, *refs = refs
+    w_refs, (others_ref, spread_ref, rt_ref, all_ref) = refs[: g.D], refs[g.D :]
     row, col, depth = (lax.axis_index(a) for a in ("row", "col", "depth"))
     rows, deep = g.SP * g.I, 2 * g.QL
     for k, ref in zip((0, *g.order), x_refs, strict=True):
@@ -328,7 +328,7 @@
 
 
 def own_kernel(
-    g, xall_ref, d_ref, ts_ref, w1_ref, w2_ref, mask_ref, part_ref, gg_ref, gate_weight_ref, own_ref,
+    g, xall_ref, near_ref, d_ref, ts_ref, w1_ref, w2_ref, mask_ref, part_ref, gg_ref, gate_weight_ref, own_ref,
     spread_ref, rt_ref, ds_ref, turn_ref,
 ):
     scale = mask_ref[g.C * g.SP : g.C * g.SP + 1, :]
@@ -353,17 +353,22 @@
             rt_ref[q * g.S : (q + 1) * g.S, t * LANES : t * LANES + lanes] = rows_of(halves)[
                 :, :lanes
             ].astype(BF16)
-    rt = rt_ref[...]
-    for i in range(0, g.I, 2):
-        product = mm(rt, lanes_of([d_ref[i], d_ref[i + 1]]))
-        for k in range(2):
-            block = product[:, k * g.Z : (k + 1) * g.Z]
-            ds_ref[:, i + k] = block.reshape(g.Q, g.S, g.Z).astype(BF16)
+    col = lax.axis_index("col")
     entries = g.S * g.I
     left_grad = jnp.zeros((entries, g.Q), F32)
-    for q in range(0, g.Q, 2):
-        both = lanes_of([ds_ref[q].reshape(entries, g.Z), ds_ref[q + 1].reshape(entries, g.Z)])
-        left_grad = left_grad + mm(both, lanes_of([ts_ref[q], ts_ref[q + 1]]), NT)
+    for m in range(g.C):
+        first = lax.rem(col + m, g.C) * g.QL
+        if m > 0:
+            rt = rt_ref[pl.ds(pl.multiple_of(first * g.S, g.QL * g.S), g.QL * g.S), :]
+            for i in range(0, g.I, 2):
+                product = mm(rt, lanes_of([d_ref[i], d_ref[i + 1]]))
+                for k in range(2):
+                    block = product[:, k * g.Z : (k + 1) * g.Z]
+                    ds_ref[m - 1, :, i + k] = block.reshape(g.QL, g.S, g.Z).astype(BF16)
+        for q in range(0, g.QL, 2):
+            pair = [near_ref[q + k, 0] if m == 0 else ds_ref[m - 1, q + k] for k in range(2)]
+            both = lanes_of([part.reshape(entries, g.Z) for part in pair])
+            left_grad = left_grad + mm(both, lanes_of([ts_ref[first + q], ts_ref[first + q + 1]]), NT)
     w1 = w1_ref[...]
     first_term = jnp.zeros((entries, 2 * g.M), F32)
     for piece in split_high_low(left_grad * scale[:, : g.Q]):
@@ -445,15 +450,18 @@
     refs = list(refs)
     sums, refs = refs[: g.R - 1], refs[g.R - 1 :]
     parts, refs = refs[: g.D], refs[g.D :]
-    outs, own_ref = refs[: g.R - 1], refs[g.R - 1]
+    outs, (own_ref, halves_ref) = refs[: g.R - 1], refs[g.R - 1 :]
+    row = lax.axis_index("row")
     total = parts[0][...]
     for ref in parts[1:]:
         total = total + ref[...]
-    total, rows = total.astype(BF16), g.SP * g.I
-    own_ref[...] = total
+    half, rows = own_ref.shape[0], g.SP * g.I
+    for k in range(2):
+        halves_ref[k] = total[k * half : (k + 1) * half].astype(BF16)
+    own_ref[...] = halves_ref[lax.rem(row, 2)]
     for x in range(1, g.R):
         outs[x - 1][:rows, :] = sums[x - 1][...]
-        outs[x - 1][rows:, :] = total
+        outs[x - 1][rows:, :] = halves_ref[lax.rem(jnp.bitwise_xor(row, x), 2)]
 
 
 def piece_kernel(g, own_ref, *refs):
@@ -528,9 +536,10 @@
 
 def across_kernel(g, *refs):
     out_ref = refs[-1]
-    col = lax.axis_index("col")
-    for k, ref in enumerate(refs[:-1]):
-        out_ref[lax.rem(col - k + g.C, g.C)] = ref[...]
+    row, col = lax.axis_index("row"), lax.axis_index("col")
+    for ref, (b, k) in zip(refs[:-1], g.spread, strict=True):
+        half = lax.rem(jnp.bitwise_xor(row, b), 2)
+        out_ref[lax.rem(col - k + g.C, g.C), half] = ref[...]
 
 
 def unpack_kernel(g, *refs):
@@ -570,7 +579,8 @@
         self.G = max(1, LANES // self.JC)
         self.EXTRA = -(-(self.C - 1) * self.S * self.QL // LANES)
         self.carried = 0
-        self.order = [*range(self.R // 2, self.R), *range(1, self.R // 2)]
+        self.spread = [(b, k) for k in range(self.C) for b in range(2)]
+        self.order = [*range(1, self.R // 2), *range(self.R // 2 + 1, self.R), self.R // 2]
 
     def fill(self, rows):
         if self.SQ == self.S:
@@ -593,6 +603,12 @@
 
 def swapped(arrays, axis):
     return [swap(a, axis, k + 1) for k, a in reversed([*enumerate(arrays)])]
+
+
+def from_near(array, b, k):
+    count, wide = lax.axis_size("row"), lax.axis_size("col")
+    pairs = [(r * wide + c, (r ^ b) * wide + (c + k) % wide) for r in range(count) for c in range(wide)]
+    return lax.ppermute(array, ("row", "col"), pairs)
 
 
 def shifted_all(array, axis):
@@ -740,16 +756,19 @@
         us=0.01,
     )
     share = g.Q * g.QL // g.D
-    xall, *matrix_parts = call(
+    xall, products, *matrix_parts = call(
         outer_kernel,
         "outer",
         (*everyone, cotangents, left, w2, masks),
-        [pltpu.VMEM((g.SP, g.N, 2 * g.M), BF16)] + [pltpu.VMEM((share, g.Z), F32)] * g.D,
+        [
+            pltpu.VMEM((g.SP, g.N, 2 * g.M), BF16),
+            pltpu.VMEM((g.QL, g.C, g.I, g.S, g.Z), BF16),
+        ]
+        + [pltpu.VMEM((share, g.Z), F32)] * g.D,
         [
             pltpu.VMEM((g.N, max(1, g.EXTRA) * LANES), BF16),
             pltpu.VMEM((g.NT, g.C * g.SP * 2 * g.QL, LANES), F32),
             pltpu.VMEM((g.QL * g.C * g.S, g.N), BF16),
-            pltpu.VMEM((g.QL, g.C, g.I, g.S, g.Z), BF16),
             pltpu.VMEM((g.Q * g.QL, g.Z), F32),
         ],
         after=(second_term,),
@@ -776,7 +795,9 @@
         pack_kernel,
         "pack",
         (*sums, *matrix_parts),
-        [pltpu.VMEM((rows + share, 2 * g.M), BF16)] * (g.R - 1) + [pltpu.VMEM((share, g.Z), BF16)],
+        [pltpu.VMEM((rows + share // 2, 2 * g.M), BF16)] * (g.R - 1)
+        + [pltpu.VMEM((share // 2, g.Z), BF16)],
+        [pltpu.VMEM((2, share // 2, g.Z), BF16)],
         us=0.2,
     )
     sums = swapped(sums, "row")
@@ -794,12 +815,12 @@
     own = call(
         own_kernel,
         "own",
-        (xall, cotangents, weights, w1, w2, masks, own, gate_grads, gate_weights),
+        (xall, products, cotangents, weights, w1, w2, masks, own, gate_grads, gate_weights),
         [pltpu.VMEM((rows, 2 * g.M), F32)],
         [
             pltpu.VMEM((g.NT, g.SP * 2 * g.Q, LANES), F32),
             pltpu.VMEM((g.Q * g.S, g.N), BF16),
-            pltpu.VMEM((g.Q, g.I, g.S, g.Z), BF16),
+            pltpu.VMEM((max(1, g.C - 1), g.QL, g.I, g.S, g.Z), BF16),
             pltpu.VMEM((g.I * g.S, 2 * g.M), F32),
         ],
         after=(scores,),
@@ -809,12 +830,12 @@
         piece_kernel,
         "piece",
         (piece, *sums),
-        [pltpu.VMEM((share, g.Z), BF16)],
-        [pltpu.VMEM((g.R, share, g.Z), BF16)],
+        [pltpu.VMEM((share // 2, g.Z), BF16)],
+        [pltpu.VMEM((g.R, share // 2, g.Z), BF16)],
         after=(own,),
         us=0.1,
     )
-    pieces = shifted_all(piece, "col")
+    pieces = [piece] + [from_near(piece, b, k) for b, k in g.spread[1:]]
     part = call(
         reduce_kernel,
         "reduce",
@@ -834,7 +855,7 @@
         across_kernel,
         "across",
         pieces,
-        [pltpu.VMEM((g.C, share, g.Z), BF16)],
+        [pltpu.VMEM((g.C, 2, share // 2, g.Z), BF16)],
         after=(pairwise_gradient,),
         distant=True,
         us=0.1,

time: 36.4 us -> 36.2 us (level)
  starting transfers between devices: 14.5 us -> 16.8 us
  waiting for transfers between devices: 6.19 us -> 4.55 us
  Pallas kernels: 14.7 us -> 13.8 us
    ppermute x0 -> x3, starting transfers between devices: none -> 3.55 us  [from_near(): return lax.ppermute(array, ('row', 'col'), pairs)]
    ppermute x6, waiting for transfers between devices: 3.48 us -> 2.02 us  [swap(): lax.ppermute(array, axis, [(i, i ^ x) for i in range(lax.axis_size(axis))])]
    ppermute x7 -> x6, starting transfers between devices: 5.92 us -> 4.64 us  [shift(): lax.ppermute(array, axis, [(i, (i + k) % count) for i in range(count)])]
    pallas_call x15, Pallas kernels: 14.7 us -> 13.8 us  [call(): pl.pallas_call(body, out_shape=outs[0] if single else tuple(outs), in_spe...]
    ppermute x7 -> x6, waiting for transfers between devices: 2.71 us -> 2.52 us  [shift(): lax.ppermute(array, axis, [(i, (i + k) % count) for i in range(count)])]
  transfers between devices with their start and end apart: 13 -> 15, of which waited for: 6 -> 4; matrix products, arithmetic and copies ran while one was open for 0% -> 0% of each run, Pallas kernels for 28% -> 26%
where the time goes in v3:
time: 36.2 us; the launch traced here: 36 us
  starting transfers between devices  16.8 us (46%)
  Pallas kernels  13.8 us (38%)
  waiting for transfers between devices  4.55 us (13%)
  between operations  0.79 us (2%)
    pallas_call x15, Pallas kernels, call(): pl.pallas_call(body, out_shape=outs[0] if single else tuple(outs), in_spe...  13.8 us
    ppermute x6, starting transfers between devices, swap(): lax.ppermute(array, axis, [(i, i ^ x) for i in range(lax.axis_size(axis))])  8.62 us
    ppermute x6, starting transfers between devices, shift(): lax.ppermute(array, axis, [(i, (i + k) % count) for i in range(count)])  4.64 us
    ppermute x3, starting transfers between devices, from_near(): return lax.ppermute(array, ('row', 'col'), pairs)  3.55 us
    ppermute x6, waiting for transfers between devices, shift(): lax.ppermute(array, axis, [(i, (i + k) % count) for i in range(count)])  2.52 us
    ppermute x6, waiting for transfers between devices, swap(): lax.ppermute(array, axis, [(i, i ^ x) for i in range(lax.axis_size(axis))])  2.02 us
  transfers between devices with their start and end apart: 15, of which 4 were waited for; matrix products, arithmetic and copies ran while one was open for 0% of the time, Pallas kernels for 26%

profile of v3, /device:TPU:0, one launch (start us, length us, event | category | flops | bytes accessed | tf_op | source)
XLA Modules:
  0.0 36.0 jit_solution(15652637914329176941)
XLA Ops:
  0.6 1.9 %normalise.1 = (bf16[2,8,16,128]{3,2,1,0:T(8,128)(2,1)S(1)}, bf16[160,128]{1,0:T(8,128)(2,1)S(1)}, f32[32,128]{1,0:T(8,128)S(1)}, bf16[608,128]{1,0:T(8,128)(2,1...) custom-call(bf16[32,16,64]{2,1,0:T(8,128)(2,1)} %refs_0_.1, ...), custom_call_target="tpu_custom_call" | custom-call | flops 2300000000 | bytes 1327744 | tf_op jit(solution)/shard_map/normalise/pallas_call | solution.py:652
  2.5 3.0 %collective-permute-start.3 = (bf16[608,128]{1,0:T(8,128)(2,1)S(1)}, bf16[608,128]{1,0:T(8,128)(2,1)S(1)}, u32[]{:S(2)}, u32[]{:S(2)}) collective-permute-start(bf16[608,128]{1,0:T(8,128)(2,1)S(1)} %get-tuple-element.47.refs_0_), channel_id=1, source_target_pairs={{0,2},{2,0},{1,3},{3,1},{4,6},{6,4},{5,7},{7,5},{8,10},{10,8},{9,1... | collective-permute-start | bytes 466952 | tf_op jit(solution)/shard_map/ppermute | solution.py:597
  5.5 2.6 %collective-permute-start.2 = (bf16[160,128]{1,0:T(8,128)(2,1)S(1)}, bf16[160,128]{1,0:T(8,128)(2,1)S(1)}, u32[]{:S(2)}, u32[]{:S(2)}) collective-permute-start(bf16[160,128]{1,0:T(8,128)(2,1)S(1)} %get-tuple-element.46.refs_0_), channel_id=1, source_target_pairs={{0,8},{4,12},{8,0},{12,4},{1,9},{5,13},{9,1},{13,5},{2,10},{6,14},... | collective-permute-start | bytes 122888 | tf_op jit(solution)/shard_map/ppermute | solution.py:601
  8.1 1.3 %collective-permute-start.1 = (bf16[160,128]{1,0:T(8,128)(2,1)S(1)}, bf16[160,128]{1,0:T(8,128)(2,1)S(1)}, u32[]{:S(2)}, u32[]{:S(2)}) collective-permute-start(bf16[160,128]{1,0:T(8,128)(2,1)S(1)} %get-tuple-element.46.refs_0_), channel_id=1, source_target_pairs={{0,12},{4,8},{8,4},{12,0},{1,13},{5,9},{9,5},{13,1},{2,14},{6,10},... | collective-permute-start | bytes 122888 | tf_op jit(solution)/shard_map/ppermute | solution.py:601
  9.4 0.2 collective-permute-start
  9.7 1.5 %prepare.1 = (bf16[512,32]{1,0:T(8,128)(2,1)S(1)}, bf16[32,32,128]{2,1,0:T(8,128)(2,1)S(1)}, bf16[16,512,128]{2,1,0:T(8,128)(2,1)S(1)}, bf16[16,16,64]{2,1,0:T(8...) custom-call(bf16[2,8,16,128]{3,2,1,0:T(8,128)(2,1)S(1)} %get-tuple-element.48., ...), custom_call_target="tpu_custom_call" | custom-call | flops 11500000 | bytes 3031040 | tf_op jit(solution)/shard_map/prepare/pallas_call | solution.py:652
  11.2 0.0 collective-permute-done.3.refs_4_.refs_1_.refs_2_
  11.2 0.2 gate.1
  11.4 1.1 %right.1 = (bf16[16,64,128]{2,1,0:T(8,128)(2,1)S(1)}, f32[8,64,128]{2,1,0:T(8,128)S(1)}) custom-call(bf16[608,128]{1,0:T(8,128)(2,1)S(1)} %get-tuple-element.47.refs_0_, bf16[608,128]{1,0:T(8,128)(2,1)S(1)} %collective-permute-done.3.refs_4_.refs_1_.refs_2_, bf16[16,512,128]{2,1,0:T(8,128)(2,1)S(1)} %get-tuple-element.52.refs_2_, ...), custom_call_target="tpu_custom_call" | custom-call | flops 11500000 | bytes 2949120 | tf_op jit(solution)/shard_map/right/pallas_call | solution.py:652
  12.6 0.0 collective-permute-done.2.refs_3_
  12.6 1.3 %collective-permute-done.1.refs_2_ = bf16[160,128]{1,0:T(8,128)(2,1)S(1)} collective-permute-done((bf16[160,128]{1,0:T(8,128)(2,1)S(1)}, bf16[160,128]{1,0:T(8,128)(2,1)S(1)}, u32[]{:S(2)}, u32[]{:S(2)}) %collective-permute-start.1) | collective-permute-done | bytes 40992 | tf_op jit(solution)/shard_map/ppermute | solution.py:601
  13.9 1.6 %outer.1 = (bf16[8,64,128]{2,1,0:T(8,128)(2,1)S(1)}, bf16[16,2,16,16,128]{4,3,2,1,0:T(8,128)(2,1)S(1)}, f32[256,128]{1,0:T(8,128)S(1)}, f32[256,128]{1,0:T(8,128)S(1)}) custom-call(bf16[160,128]{1,0:T(8,128)(2,1)S(1)} %get-tuple-element.46.refs_0_, bf16[160,128]{1,0:T(8,128)(2,1)S(1)} %collective-permute-done.refs_1_, ...), custom_call_target="tpu_custom_call" | custom-call | flops 57500000 | bytes 2965504 | tf_op jit(solution)/shard_map/outer/pallas_call | solution.py:652
  15.5 0.1 collective-permute-start.5
  15.6 2.2 %attend.1 = (f32[128,64]{1,0:T(8,128)S(1)}, f32[128,64]{1,0:T(8,128)S(1)}, f32[128,128]{1,0:T(8,128)S(1)}, bf16[128,512]{1,0:T(8,128)(2,1)S(1)}, bf16[128,128]{1...) custom-call(bf16[8,64,128]{2,1,0:T(8,128)(2,1)S(1)} %get-tuple-element.61.refs_0_, ...), custom_call_target="tpu_custom_call" | custom-call | flops 3449999872 | bytes 1351680 | tf_op jit(solution)/shard_map/attend/pallas_call | solution.py:652
  17.9 2.1 %collective-permute-start.6 = (bf16[256,128]{1,0:T(8,128)(2,1)S(1)}, bf16[256,128]{1,0:T(8,128)(2,1)S(1)}, u32[]{:S(2)}, u32[]{:S(2)}) collective-permute-start(bf16[256,128]{1,0:T(8,128)(2,1)S(1)} %get-tuple-element.79), channel_id=1, source_target_pairs={{0,12},{4,8},{8,4},{12,0},{1,13},{5,9},{9,5},{13,1},{2,14},{6,10},... | collective-permute-start | bytes 196616 | tf_op jit(solution)/shard_map/ppermute | solution.py:601
  19.9 0.0 collective-permute-start.7
  20.0 2.4 %collective-permute-start.8 = (bf16[256,128]{1,0:T(8,128)(2,1)S(1)}, bf16[256,128]{1,0:T(8,128)(2,1)S(1)}, u32[]{:S(2)}, u32[]{:S(2)}) collective-permute-start(bf16[256,128]{1,0:T(8,128)(2,1)S(1)} %get-tuple-element.81), channel_id=1, source_target_pairs={{0,4},{4,0},{8,12},{12,8},{1,5},{5,1},{9,13},{13,9},{2,6},{6,2},{1... | collective-permute-start | bytes 196616 | tf_op jit(solution)/shard_map/ppermute | solution.py:601
  22.3 1.3 %collective-permute-done.4.refs_2_ = f32[128,64]{1,0:T(8,128)S(1)} collective-permute-done((f32[128,64]{1,0:T(8,128)S(1)}, f32[128,64]{1,0:T(8,128)S(1)}, u32[]{:S(2)}, u32[]{:S(2)}) %collective-permute-start.4) | collective-permute-done | bytes 32800 | tf_op jit(solution)/shard_map/ppermute | solution.py:597
  23.6 0.2 score.1
  23.8 0.6 %collective-permute-start.13 = (bf16[128,128]{1,0:T(8,128)(2,1)S(1)}, bf16[128,128]{1,0:T(8,128)(2,1)S(1)}, u32[]{:S(2)}, u32[]{:S(2)}) collective-permute-start(bf16[128,128]{1,0:T(8,128)(2,1)S(1)} %get-tuple-element.84), channel_id=1, source_target_pairs={{0,2},{2,0},{1,3},{3,1},{4,6},{6,4},{5,7},{7,5},{8,10},{10,8},{9,1... | collective-permute-start | bytes 98312 | tf_op jit(solution)/shard_map/ppermute | solution.py:597
  24.4 1.9 %own.1.refs_4_.refs_1_ = f32[128,128]{1,0:T(8,128)S(1)} custom-call(bf16[8,64,128]{2,1,0:T(8,128)(2,1)S(1)} %get-tuple-element.61.refs_0_, bf16[16,2,16,16,128]{4,3,2,1,0:T(8,128)(2,1)S(1)} %get-tuple-element.62.refs_1_, bf16[16,64,128]{2,1,0:T(8,128)(2,1)S(1)} %get-tuple-element.58.refs_4_.refs_2_, bf16[32,32,128]{2,1,0:T(8,128)(2,1)S(1)} %get-tuple-element.63.refs_3_, ...), custom_call_target="tpu_custom_call" | custom-call | flops 11500000 | bytes 3166208 | tf_op jit(solution)/shard_map/own/pallas_call | solution.py:652
  26.3 0.7 %collective-permute-done.7.refs_2_.refs_3_ = bf16[256,128]{1,0:T(8,128)(2,1)S(1)} collective-permute-done((bf16[256,128]{1,0:T(8,128)(2,1)S(1)}, bf16[256,128]{1,0:T(8,128)(2,1)S(1)}, u32[]{:S(2)}, u32[]{:S(2)}) %collective-permute-start.7) | collective-permute-done | bytes 65568 | tf_op jit(solution)/shard_map/ppermute | solution.py:601
  27.1 0.3 collective-permute-start.12
  27.4 1.5 %collective-permute-start.11 = (bf16[128,128]{1,0:T(8,128)(2,1)S(1)}, bf16[128,128]{1,0:T(8,128)(2,1)S(1)}, u32[]{:S(2)}, u32[]{:S(2)}) collective-permute-start(bf16[128,128]{1,0:T(8,128)(2,1)S(1)} %piece.1.refs_5_.refs_0_), channel_id=1, source_target_pairs={{0,2},{2,0},{4,6},{6,4},{8,10},{10,8},{12,14},{14,12},{1,3},{3,1},... | collective-permute-start | bytes 98312 | tf_op jit(solution)/shard_map/ppermute | solution.py:611
  28.9 1.8 %collective-permute-start.10 = (bf16[128,128]{1,0:T(8,128)(2,1)S(1)}, bf16[128,128]{1,0:T(8,128)(2,1)S(1)}, u32[]{:S(2)}, u32[]{:S(2)}) collective-permute-start(bf16[128,128]{1,0:T(8,128)(2,1)S(1)} %piece.1.refs_5_.refs_0_), channel_id=1, source_target_pairs={{0,4},{2,6},{4,0},{6,2},{8,12},{10,14},{12,8},{14,10},{1,5},{3,7},... | collective-permute-start | bytes 98312 | tf_op jit(solution)/shard_map/ppermute | solution.py:611
  30.6 0.4 %reduce.1.refs_5_.refs_0_ = bf16[128,128]{1,0:T(8,128)(2,1)S(1)} custom-call(bf16[16,16,64]{2,1,0:T(8,128)(2,1)S(1)} %get-tuple-element.45.refs_0_, f32[128,128]{1,0:T(8,128)S(1)} %own.1.refs_4_.refs_1_, bf16[256,128]{1,0:T(8,128)(2,1)S(1)} %collective-permute-done.6.refs_1_.refs_2_, bf16[256,128]{1,0:T(8,128)(2,1)S(1)} %collective-permute-done.7.refs_2_.refs_3_, ...), custom_call_target="tpu_custom_call" | custom-call | flops 1150000000 | bytes 327680 | tf_op jit(solution)/shard_map/reduce/pallas_call | solution.py:652
  31.0 0.9 %collective-permute-start.9 = (bf16[128,128]{1,0:T(8,128)(2,1)S(1)}, bf16[128,128]{1,0:T(8,128)(2,1)S(1)}, u32[]{:S(2)}, u32[]{:S(2)}) collective-permute-start(bf16[128,128]{1,0:T(8,128)(2,1)S(1)} %reduce.1.refs_5_.refs_0_), channel_id=1, source_target_pairs={{0,2},{2,0},{1,3},{3,1},{4,6},{6,4},{5,7},{7,5},{8,10},{10,8},{9,1... | collective-permute-start | bytes 98312 | tf_op jit(solution)/shard_map/ppermute | solution.py:597
  31.9 1.7 %pair.1.refs_4_ = bf16[16,32,128]{2,1,0:T(8,128)(2,1)} custom-call(bf16[16,32,128]{2,1,0:T(8,128)(2,1)S(1)} %get-tuple-element.82.refs_0_, bf16[8,128]{1,0:T(8,128)(2,1)S(1)} %get-tuple-element.83.refs_1_, f32[128,64]{1,0:T(8,128)S(1)} %get-tuple-element.70.refs_0_.refs_2_, f32[128,33]{1,0:T(8,128)S(1)} %get-tuple-element.78.refs_10_.refs_3_, ...), custom_call_target="tpu_custom_call" | custom-call | flops 11500000 | bytes 346624 | tf_op jit(solution)/shard_map/pair/pallas_call | solution.py:652
  33.6 0.1 collective-permute-start.14
  33.7 1.3 %collective-permute-done.9.refs_1_ = bf16[128,128]{1,0:T(8,128)(2,1)S(1)} collective-permute-done((bf16[128,128]{1,0:T(8,128)(2,1)S(1)}, bf16[128,128]{1,0:T(8,128)(2,1)S(1)}, u32[]{:S(2)}, u32[]{:S(2)}) %collective-permute-start.9) | collective-permute-done | bytes 32800 | tf_op jit(solution)/shard_map/ppermute | solution.py:597
  35.0 0.1 unpack.1.refs_0_
  35.1 0.9 %finish.1 = (bf16[32,16,64]{2,1,0:T(8,128)(2,1)}, f32[32,32,128]{2,1,0:T(8,128)}) custom-call(bf16[32,16,64]{2,1,0:T(8,128)(2,1)S(1)} %unpack.1.refs_0_, bf16[2,16,16,128]{3,2,1,0:T(8,128)(2,1)S(1)} %bitcast.11, bf16[2,16,16,128]{3,2,1,0:T(8,128)(2,1)S(1)} %collective-permute-done.14.refs_2_), custom_call_target="tpu_custom_call" | custom-call | flops 1150000000 | bytes 917504 | tf_op jit(solution)/shard_map/finish/pallas_call | solution.py:652
  (13 shorter events, 0.1 us)
Async XLA Ops:
  2.5 8.7 %collective-permute-start.3 = (bf16[608,128]{1,0:T(8,128)(2,1)S(1)}, bf16[608,128]{1,0:T(8,128)(2,1)S(1)}, u32[]{:S(2)}, u32[]{:S(2)}) collective-permute-start(bf16[608,128]{1,0:T(8,128)(2,1)S(1)} %get-tuple-element.47.refs_0_), channel_id=1, source_target_pairs={{0,2},{2,0},{1,3},{3,1},{4,6},{6,4},{5,7},{7,5},{8,10},{10,8},{9,1... | collective-permute-start | bytes 466952 | tf_op jit(solution)/shard_map/ppermute | solution.py:597
  5.5 7.1 %collective-permute-start.2 = (bf16[160,128]{1,0:T(8,128)(2,1)S(1)}, bf16[160,128]{1,0:T(8,128)(2,1)S(1)}, u32[]{:S(2)}, u32[]{:S(2)}) collective-permute-start(bf16[160,128]{1,0:T(8,128)(2,1)S(1)} %get-tuple-element.46.refs_0_), channel_id=1, source_target_pairs={{0,8},{4,12},{8,0},{12,4},{1,9},{5,13},{9,1},{13,5},{2,10},{6,14},... | collective-permute-start | bytes 122888 | tf_op jit(solution)/shard_map/ppermute | solution.py:601
  8.1 5.8 %collective-permute-start.1 = (bf16[160,128]{1,0:T(8,128)(2,1)S(1)}, bf16[160,128]{1,0:T(8,128)(2,1)S(1)}, u32[]{:S(2)}, u32[]{:S(2)}) collective-permute-start(bf16[160,128]{1,0:T(8,128)(2,1)S(1)} %get-tuple-element.46.refs_0_), channel_id=1, source_target_pairs={{0,12},{4,8},{8,4},{12,0},{1,13},{5,9},{9,5},{13,1},{2,14},{6,10},... | collective-permute-start | bytes 122888 | tf_op jit(solution)/shard_map/ppermute | solution.py:601
  9.4 4.5 %collective-permute-start = (bf16[160,128]{1,0:T(8,128)(2,1)S(1)}, bf16[160,128]{1,0:T(8,128)(2,1)S(1)}, u32[]{:S(2)}, u32[]{:S(2)}) collective-permute-start(bf16[160,128]{1,0:T(8,128)(2,1)S(1)} %get-tuple-element.46.refs_0_), channel_id=1, source_target_pairs={{0,4},{4,0},{8,12},{12,8},{1,5},{5,1},{9,13},{13,9},{2,6},{6,2},{1... | collective-permute-start | bytes 122888 | tf_op jit(solution)/shard_map/ppermute | solution.py:601
  15.5 2.3 %collective-permute-start.5 = (f32[256,128]{1,0:T(8,128)S(1)}, f32[256,128]{1,0:T(8,128)S(1)}, u32[]{:S(2)}, u32[]{:S(2)}) collective-permute-start(f32[256,128]{1,0:T(8,128)S(1)} %get-tuple-element.76), channel_id=1, source_target_pairs={{0,1},{1,0},{2,3},{3,2},{4,5},{5,4},{6,7},{7,6},{8,9},{9,8},{10,11... | collective-permute-start | bytes 393224 | tf_op jit(solution)/shard_map/ppermute | solution.py:597
  17.9 8.5 %collective-permute-start.6 = (bf16[256,128]{1,0:T(8,128)(2,1)S(1)}, bf16[256,128]{1,0:T(8,128)(2,1)S(1)}, u32[]{:S(2)}, u32[]{:S(2)}) collective-permute-start(bf16[256,128]{1,0:T(8,128)(2,1)S(1)} %get-tuple-element.79), channel_id=1, source_target_pairs={{0,12},{4,8},{8,4},{12,0},{1,13},{5,9},{9,5},{13,1},{2,14},{6,10},... | collective-permute-start | bytes 196616 | tf_op jit(solution)/shard_map/ppermute | solution.py:601
  19.9 7.1 %collective-permute-start.7 = (bf16[256,128]{1,0:T(8,128)(2,1)S(1)}, bf16[256,128]{1,0:T(8,128)(2,1)S(1)}, u32[]{:S(2)}, u32[]{:S(2)}) collective-permute-start(bf16[256,128]{1,0:T(8,128)(2,1)S(1)} %get-tuple-element.80), channel_id=1, source_target_pairs={{0,8},{4,12},{8,0},{12,4},{1,9},{5,13},{9,1},{13,5},{2,10},{6,14},... | collective-permute-start | bytes 196616 | tf_op jit(solution)/shard_map/ppermute | solution.py:601
  20.0 7.1 %collective-permute-start.8 = (bf16[256,128]{1,0:T(8,128)(2,1)S(1)}, bf16[256,128]{1,0:T(8,128)(2,1)S(1)}, u32[]{:S(2)}, u32[]{:S(2)}) collective-permute-start(bf16[256,128]{1,0:T(8,128)(2,1)S(1)} %get-tuple-element.81), channel_id=1, source_target_pairs={{0,4},{4,0},{8,12},{12,8},{1,5},{5,1},{9,13},{13,9},{2,6},{6,2},{1... | collective-permute-start | bytes 196616 | tf_op jit(solution)/shard_map/ppermute | solution.py:601
  22.3 1.3 %collective-permute-start.4 = (f32[128,64]{1,0:T(8,128)S(1)}, f32[128,64]{1,0:T(8,128)S(1)}, u32[]{:S(2)}, u32[]{:S(2)}) collective-permute-start(f32[128,64]{1,0:T(8,128)S(1)} %get-tuple-element.71.refs_1_), channel_id=1, source_target_pairs={{0,1},{1,0},{2,3},{3,2},{4,5},{5,4},{6,7},{7,6},{8,9},{9,8},{10,11... | collective-permute-start | bytes 98312 | tf_op jit(solution)/shard_map/ppermute | solution.py:597
  23.8 8.1 %collective-permute-start.13 = (bf16[128,128]{1,0:T(8,128)(2,1)S(1)}, bf16[128,128]{1,0:T(8,128)(2,1)S(1)}, u32[]{:S(2)}, u32[]{:S(2)}) collective-permute-start(bf16[128,128]{1,0:T(8,128)(2,1)S(1)} %get-tuple-element.84), channel_id=1, source_target_pairs={{0,2},{2,0},{1,3},{3,1},{4,6},{6,4},{5,7},{7,5},{8,10},{10,8},{9,1... | collective-permute-start | bytes 98312 | tf_op jit(solution)/shard_map/ppermute | solution.py:597
  27.1 6.5 %collective-permute-start.12 = (bf16[128,128]{1,0:T(8,128)(2,1)S(1)}, bf16[128,128]{1,0:T(8,128)(2,1)S(1)}, u32[]{:S(2)}, u32[]{:S(2)}) collective-permute-start(bf16[128,128]{1,0:T(8,128)(2,1)S(1)} %piece.1.refs_5_.refs_0_), channel_id=1, source_target_pairs={{0,6},{2,4},{4,2},{6,0},{8,14},{10,12},{12,10},{14,8},{1,7},{3,5},... | collective-permute-start | bytes 98312 | tf_op jit(solution)/shard_map/ppermute | solution.py:611
  27.4 6.2 %collective-permute-start.11 = (bf16[128,128]{1,0:T(8,128)(2,1)S(1)}, bf16[128,128]{1,0:T(8,128)(2,1)S(1)}, u32[]{:S(2)}, u32[]{:S(2)}) collective-permute-start(bf16[128,128]{1,0:T(8,128)(2,1)S(1)} %piece.1.refs_5_.refs_0_), channel_id=1, source_target_pairs={{0,2},{2,0},{4,6},{6,4},{8,10},{10,8},{12,14},{14,12},{1,3},{3,1},... | collective-permute-start | bytes 98312 | tf_op jit(solution)/shard_map/ppermute | solution.py:611
  28.9 4.7 %collective-permute-start.10 = (bf16[128,128]{1,0:T(8,128)(2,1)S(1)}, bf16[128,128]{1,0:T(8,128)(2,1)S(1)}, u32[]{:S(2)}, u32[]{:S(2)}) collective-permute-start(bf16[128,128]{1,0:T(8,128)(2,1)S(1)} %piece.1.refs_5_.refs_0_), channel_id=1, source_target_pairs={{0,4},{2,6},{4,0},{6,2},{8,12},{10,14},{12,8},{14,10},{1,5},{3,7},... | collective-permute-start | bytes 98312 | tf_op jit(solution)/shard_map/ppermute | solution.py:611
  31.0 4.0 %collective-permute-start.9 = (bf16[128,128]{1,0:T(8,128)(2,1)S(1)}, bf16[128,128]{1,0:T(8,128)(2,1)S(1)}, u32[]{:S(2)}, u32[]{:S(2)}) collective-permute-start(bf16[128,128]{1,0:T(8,128)(2,1)S(1)} %reduce.1.refs_5_.refs_0_), channel_id=1, source_target_pairs={{0,2},{2,0},{1,3},{3,1},{4,6},{6,4},{5,7},{7,5},{8,10},{10,8},{9,1... | collective-permute-start | bytes 98312 | tf_op jit(solution)/shard_map/ppermute | solution.py:597
  33.6 1.4 %collective-permute-start.14 = (bf16[2,16,16,128]{3,2,1,0:T(8,128)(2,1)S(1)}, bf16[2,16,16,128]{3,2,1,0:T(8,128)(2,1)S(1)}, u32[]{:S(2)}, u32[]{:S(2)}) collective-permute-start(bf16[2,16,16,128]{3,2,1,0:T(8,128)(2,1)S(1)} %bitcast.9), channel_id=1, source_target_pairs={{0,1},{1,0},{2,3},{3,2},{4,5},{5,4},{6,7},{7,6},{8,9},{9,8},{10,11... | collective-permute-start | bytes 393224 | tf_op jit(solution)/shard_map/ppermute | solution.py:597
